TPU v7x, 32 devices: a whole 2x2x4 slice. The times are simulated.
32 devices in a mesh: dp: 8 (over y, x, core), mp: 4 (over z).
Axes of the slice: x: 2, y: 2, z: 4, core: 2. Of those that a mesh axis runs over, the one named last changes fastest.
Arguments:
- query_tokens: bfloat16 [8, 257, 5120], P('dp', None, 'mp'), may hold values from -200 to 200
- key_tokens: bfloat16 [8, 257, 5120], P('dp', None, 'mp'), may hold values from -6.5 to 6.5
- value_tokens: bfloat16 [8, 257, 5120], P('dp', None, 'mp'), may hold values from -6 to 6
- head_weight: bfloat16 [5120, 1024], P('mp', 'dp'), may hold values from -0.078125 to 0.078125
- image_cache: bfloat16 [256, 1024], P(('dp', 'mp')), may hold values from -6 to 6
- text_embed: bfloat16 [256, 1024], P(('dp', 'mp')), may hold values from -6 to 6
- text_pair: int32 [256], P(('dp', 'mp')), may hold values from 0 to 255, as said below
- image_group: int32 [256], P(('dp', 'mp')), may hold values from 0 to 127
- text_group: int32 [256], P(('dp', 'mp')), may hold values from 0 to 127
- logit_scale: float32 [], replicated, may hold values from 2.6 to 2.8
- logit_bias: float32 [], replicated, may hold values from -9 to -8
Outputs:
- query_grad: bfloat16 [8, 257, 5120], P('dp', None, 'mp')
- key_grad: bfloat16 [8, 257, 5120], P('dp', None, 'mp')
- value_grad: bfloat16 [8, 257, 5120], P('dp', None, 'mp')
- image_grad: float32 [256, 1024], P(('dp', 'mp'))
- text_grad: float32 [256, 1024], P(('dp', 'mp'))
- row_loss: float32 [256], P(('dp', 'mp'))
Inputs may be any that keep to these rules, and one draw needn't show every extreme that they name: Text j is the caption of image text_pair[j]; every image has exactly one such text.
All inputs are finite; a program needn't handle non-finite values.
Results may differ from a plain program's by a relative error of at most 0.012.
Values may be sent and summed in bfloat16 or wider, within the bound.
A program may use at most 64 MiB of HBM per device.

v0:
```python
import math

import jax
import jax.numpy as jnp
from jax import lax
from jax.sharding import PartitionSpec as P

HEAD_DIM = 128


loss_scale = 8192.0


def broadcast(block, axis, owner):
    block = jnp.where(lax.axis_index(axis) == owner, block, jnp.zeros_like(block))
    return lax.psum(block, axis)


def pair_terms(left_rows, right_rows, labels, temper, offset):
    scores = lax.dot_general(
        left_rows, right_rows, (((1,), (1,)), ((), ())), preferred_element_type=jnp.float32
    )
    logits = temper * scores + offset
    signed = jnp.where(labels, 1.0, -1.0).astype(jnp.float32)
    margin = signed * logits
    losses = -jnp.sum(jax.nn.log_sigmoid(margin), axis=1)
    coeffs = (temper * (-signed * jax.nn.sigmoid(-margin))).astype(jnp.bfloat16)
    return (coeffs, losses)


def unit_rows(raw_rows):
    row_norm = lax.rsqrt(jnp.sum(raw_rows * raw_rows, axis=1, keepdims=True) + 1e-06)
    return (raw_rows * row_norm, row_norm)


def on_device(
    query_tokens,
    key_tokens,
    value_tokens,
    head_weight,
    image_cache,
    text_embed,
    text_pair,
    image_group,
    text_group,
    logit_scale,
    logit_bias,
):
    images_here, seq_len, width_here = query_tokens.shape
    heads_here = width_here // HEAD_DIM
    shaped = (images_here, seq_len, heads_here, HEAD_DIM)
    queries = query_tokens.reshape(shaped)
    key_heads = key_tokens.reshape(shaped)
    value_heads = value_tokens.reshape(shaped)
    inv_root = 1.0 / math.sqrt(HEAD_DIM)
    raw_scores = (
        jnp.einsum("bihd,bjhd->bhij", queries, key_heads, preferred_element_type=jnp.float32)
        * inv_root
    )
    attn_probs = jax.nn.softmax(raw_scores, axis=-1)
    probs_low = attn_probs.astype(jnp.bfloat16)
    attended = jnp.einsum(
        "bhij,bjhd->bihd", probs_low, value_heads, preferred_element_type=jnp.float32
    )
    pooled = jnp.mean(attended, axis=1).reshape(images_here, width_here).astype(jnp.bfloat16)
    full_weight = lax.all_gather(head_weight, "dp", axis=1, tiled=True)
    partial_value = jnp.dot(pooled, full_weight, preferred_element_type=jnp.float32)
    fresh = lax.psum(partial_value, "mp")
    mp_index = lax.axis_index("mp")
    dp_index = lax.axis_index("dp")
    rows = image_cache.shape[0]
    block = rows * lax.axis_size("mp")
    is_fresh = (jnp.arange(rows) == 0) & (mp_index == 0)
    raw_image = jnp.where(is_fresh[:, None], fresh, image_cache.astype(jnp.float32))
    unit_image, image_norm = unit_rows(raw_image)
    unit_text, text_norm = unit_rows(text_embed.astype(jnp.float32))
    image_low = unit_image.astype(jnp.bfloat16)
    text_low = unit_text.astype(jnp.bfloat16)
    group_images, group_texts, group_igroups, group_pairs, group_tgroups = (
        lax.all_gather(image_low, "mp", axis=0, tiled=True),
        lax.all_gather(text_low, "mp", axis=0, tiled=True),
        lax.all_gather(image_group, "mp", axis=0, tiled=True),
        lax.all_gather(text_pair, "mp", axis=0, tiled=True),
        lax.all_gather(text_group, "mp", axis=0, tiled=True),
    )
    group_index = dp_index * block + jnp.arange(block)
    temper = jnp.exp(logit_scale)
    piece_images = lax.all_gather(image_low, "dp", axis=0, tiled=True)
    piece_texts = lax.all_gather(text_low, "dp", axis=0, tiled=True)
    piece_igroups = lax.all_gather(image_group, "dp", axis=0, tiled=True)
    piece_pairs = lax.all_gather(text_pair, "dp", axis=0, tiled=True)
    piece_tgroups = lax.all_gather(text_group, "dp", axis=0, tiled=True)
    labels = (piece_pairs[None, :] == group_index[:, None]) | (
        group_igroups[:, None] == piece_tgroups[None, :]
    )
    coeffs, losses = pair_terms(group_images, piece_texts, labels, temper, logit_bias)
    image_part, losses = (jnp.dot(coeffs, piece_texts, preferred_element_type=jnp.float32), losses)
    count = piece_images.shape[0]
    spots = jnp.arange(count)
    piece_index = spots // rows * block + mp_index * rows + spots % rows
    labels_back = (group_pairs[:, None] == piece_index[None, :]) | (
        group_tgroups[:, None] == piece_igroups[None, :]
    )
    coeffs_back, unused = pair_terms(group_texts, piece_images, labels_back, temper, logit_bias)
    text_part = jnp.dot(coeffs_back, piece_images, preferred_element_type=jnp.float32)
    image_dir, text_dir, row_loss = (
        lax.psum_scatter(image_part, "mp", scatter_dimension=0, tiled=True),
        lax.psum_scatter(text_part, "mp", scatter_dimension=0, tiled=True),
        lax.psum_scatter(losses, "mp", scatter_dimension=0, tiled=True),
    )
    image_grad = (
        image_dir - unit_image * jnp.sum(unit_image * image_dir, axis=1, keepdims=True)
    ) * image_norm
    text_grad = (
        text_dir - unit_text * jnp.sum(unit_text * text_dir, axis=1, keepdims=True)
    ) * text_norm
    fresh_low = broadcast(image_grad[0:1].astype(jnp.bfloat16), "mp", 0)
    pooled_grad = lax.dot_general(
        fresh_low, full_weight, (((1,), (1,)), ((), ())), preferred_element_type=jnp.float32
    )
    cotangent = (
        (pooled_grad * (loss_scale / seq_len))
        .astype(jnp.bfloat16)
        .reshape(images_here, heads_here, HEAD_DIM)
    )
    prob_grad = jnp.einsum(
        "bhd,bjhd->bhj", cotangent, value_heads, preferred_element_type=jnp.float32
    )
    centre = jnp.sum(attn_probs * prob_grad[:, :, None, :], axis=-1, keepdims=True)
    score_grad = (attn_probs * (prob_grad[:, :, None, :] - centre)).astype(jnp.bfloat16)
    query_grad = (
        jnp.einsum("bhij,bjhd->bihd", score_grad, key_heads, preferred_element_type=jnp.float32)
        * inv_root
    )
    key_grad = (
        jnp.einsum("bhij,bihd->bjhd", score_grad, queries, preferred_element_type=jnp.float32)
        * inv_root
    )
    column_mass = jnp.sum(probs_low, axis=2, dtype=jnp.float32)
    value_grad = jnp.einsum("bhj,bhd->bjhd", column_mass, cotangent.astype(jnp.float32))
    out_shape = (images_here, seq_len, width_here)
    return (
        query_grad.reshape(out_shape).astype(jnp.bfloat16),
        key_grad.reshape(out_shape).astype(jnp.bfloat16),
        value_grad.reshape(out_shape).astype(jnp.bfloat16),
        image_grad,
        text_grad,
        row_loss,
    )


def solution(mesh):
    return jax.shard_map(
        on_device,
        mesh=mesh,
        in_specs=(
            P("dp", None, "mp"),
            P("dp", None, "mp"),
            P("dp", None, "mp"),
            P("mp", "dp"),
            P(("dp", "mp"), None),
            P(("dp", "mp"), None),
            P(("dp", "mp")),
            P(("dp", "mp")),
            P(("dp", "mp")),
            P(),
            P(),
        ),
        out_specs=(
            P("dp", None, "mp"),
            P("dp", None, "mp"),
            P("dp", None, "mp"),
            P(("dp", "mp"), None),
            P(("dp", "mp"), None),
            P(("dp", "mp")),
        ),
        check_vma=False,
    )
```

profile of v0, /device:TPU:0, one launch (start us, length us, event | category | flops | bytes accessed | tf_op | source)
XLA Modules:
  0.0 144.9 jit_solution(2748858110569734440)
XLA Ops:
  7.2 0.7 all-gather.2.cloned.1.call-update
  8.0 1.5 %reshape.207 = bf16[257,10,128]{2,1,0:T(8,128)(2,1)S(1)} reshape(bf16[1,257,1280]{2,1,0:T(8,128)(2,1)} %param.11) | data formatting | bytes 1315840 | tf_op jit(solution)/shard_map/reshape
  9.4 1.8 %reshape.208 = bf16[257,10,128]{2,1,0:T(8,128)(2,1)S(1)} reshape(bf16[1,257,1280]{2,1,0:T(8,128)(2,1)} %param.12) | data formatting | bytes 1315840 | tf_op jit(solution)/shard_map/reshape.1
  11.2 1.8 %reshape.209 = bf16[257,10,128]{2,1,0:T(8,128)(2,1)S(1)} reshape(bf16[1,257,1280]{2,1,0:T(8,128)(2,1)} %param.13) | data formatting | bytes 1315840 | tf_op jit(solution)/shard_map/reshape.5
  13.0 0.9 fusion.26
  13.9 3.0 %fusion.77 = (f32[10,257]{1,0:T(8,128)S(1)}, f32[10,257,257]{1,2,0:T(8,128)S(1)}) fusion(f32[10,257,257]{1,2,0:T(8,128)S(1)} %fusion.26), kind=kOutput, calls=%fused_computation.112 | output fusion | flops 2642216 | bytes 5294200 | tf_op jit(solution)/shard_map/sub | solution.py:60
  17.1 1.2 convolution_reduce_fusion
  18.3 0.6 copy-done
  18.9 0.6 dynamic-slice
  19.5 0.6 fusion.76
  21.4 0.2 dynamic-update-slice.3
  21.7 0.2 dynamic-update-slice.4
  21.9 0.2 dynamic-update-slice
  22.1 0.2 dynamic-update-slice.2
  22.3 0.2 dynamic-update-slice.1
  22.5 0.2 dynamic-update-slice.5
  24.7 9.9 %all-reduce.8 = (s32[32]{0:T(128)S(1)}, s32[32]{0:T(128)S(1)}, s32[32]{0:T(128)S(1)}) all-reduce(s32[32]{0:T(128)S(1)} %dynamic-update-slice.1, s32[32]{0:T(128)S(1)} %dynamic-update-slice.4, s32[32]{0:T(128)S(1)} %dynamic-update-slice.3), channel_id=1, replica_groups=mesh['dp'=8,'mp'=4] {'mp'}, use_global_device_ids=true, to_apply=%add.1 | all-reduce | flops 96 | bytes 768
  34.6 8.1 %all-reduce.7 = (s32[64]{0:T(128)S(1)}, s32[64]{0:T(128)S(1)}, s32[64]{0:T(128)S(1)}) all-reduce(s32[64]{0:T(128)S(1)} %dynamic-update-slice.2, s32[64]{0:T(128)S(1)} %dynamic-update-slice, s32[64]{0:T(128)S(1)} %dynamic-update-slice.5), channel_id=1, replica_groups=mesh['dp'=8,'mp'=4] {'dp'}, use_global_device_ids=true, to_apply=%add.2 | all-reduce | flops 192 | bytes 1536
  42.7 0.1 fusion.36
  42.9 13.1 %all_gather.42 = bf16[32,1024]{1,0:T(8,128)(2,1)S(1)} all-gather(bf16[8,1024]{1,0:T(8,128)(2,1)S(1)} %fusion.32), channel_id=1, replica_groups=mesh['dp'=8,'mp'=4] {'mp'}, dimensions={0}, use_global_device_ids=true | all-gather | bytes 81920 | tf_op jit(solution)/shard_map/all_gather | solution.py:81
  56.0 8.6 %all_gather.38 = bf16[64,1024]{1,0:T(8,128)(2,1)S(1)} all-gather(bf16[8,1024]{1,0:T(8,128)(2,1)S(1)} %fusion.32), channel_id=1, replica_groups=mesh['dp'=8,'mp'=4] {'dp'}, dimensions={0}, use_global_device_ids=true | all-gather | bytes 147456 | tf_op jit(solution)/shard_map/all_gather | solution.py:89
  64.7 2.3 %fusion.78 = f32[1,1024]{1,0:T(1,128)S(1)} fusion(bf16[1280,1]{0,1:T(2,128)(2,1)S(1)} %reshape.243, bf16[1280,1024]{1,0:T(8,128)(2,1)} %all-gather.2.cloned.1.call-done), kind=kOutput, calls=%fused_computation.113 | convolution fusion | flops 2621440 | bytes 2628096 | tf_op jit(solution)/shard_map/dot_general | solution.py:67
  67.0 10.0 %psum.14 = f32[1024]{0:T(1024)S(1)} all-reduce(f32[1024]{0:T(1024)S(1)} %bitcast.43), channel_id=1, replica_groups=mesh['dp'=8,'mp'=4] {'mp'}, use_global_device_ids=true, to_apply=%region_3.0 | all-reduce | flops 1024 | bytes 8192 | tf_op jit(solution)/shard_map/psum | solution.py:68
  77.0 0.2 multiply_reduce_fusion.3
  77.3 13.1 %all_gather.37 = bf16[32,1024]{1,0:T(8,128)(2,1)S(1)} all-gather(bf16[8,1024]{1,0:T(8,128)(2,1)S(1)} %fusion.38), channel_id=1, replica_groups=mesh['dp'=8,'mp'=4] {'mp'}, dimensions={0}, use_global_device_ids=true | all-gather | bytes 81920 | tf_op jit(solution)/shard_map/all_gather | solution.py:80
  90.4 0.3 fusion.43
  90.7 0.9 fusion.47
  91.7 8.7 %all-reduce.6 = f32[32]{0:T(128)S(1)} all-reduce(f32[32]{0:T(128)S(1)} %get-tuple-element.20), channel_id=4, replica_groups=mesh['dp'=8,'mp'=4] {'mp'}, use_global_device_ids=true, to_apply=%region_14.15.clone | all-reduce | flops 32 | bytes 256
  100.4 8.9 %all_gather.43 = bf16[64,1024]{1,0:T(8,128)(2,1)S(1)} all-gather(bf16[8,1024]{1,0:T(8,128)(2,1)S(1)} %fusion.38), channel_id=1, replica_groups=mesh['dp'=8,'mp'=4] {'dp'}, dimensions={0}, use_global_device_ids=true | all-gather | bytes 147456 | tf_op jit(solution)/shard_map/all_gather | solution.py:88
  109.2 1.0 fusion.19
  110.2 0.6 dynamic-slice.7
  110.8 1.0 multiply_reduce_fusion.2
  111.8 0.8 subtract_multiply_fusion
  112.7 10.2 %psum.15 = bf16[1024]{0:T(1024)(128)(2,1)S(1)} all-reduce(bf16[1024]{0:T(1024)(128)(2,1)S(1)} %fusion.65), channel_id=1, replica_groups=mesh['dp'=8,'mp'=4] {'mp'}, use_global_device_ids=true, to_apply=%region_8.9 | all-reduce | flops 1024 | bytes 4096 | tf_op jit(solution)/shard_map/psum | solution.py:16
  122.9 0.8 convolution_reduce_fusion.1
  123.7 0.4 copy-done.4
  124.1 0.3 fusion.22
  124.4 3.1 %convert_reduce_fusion = (f32[10,257]{1,0:T(8,128)S(1)}, f32[10,257]{1,0:T(8,128)S(1)}) fusion(f32[10,257,257]{1,2,0:T(8,128)} %copy-done, f32[10,257]{1,0:T(8,128)S(1)} %get-tuple-element.18, f32[10,257]{1,0:T(8,128)S(1)} %bitcast.40), kind=kLoop, calls=%fused_computation.1 | loop fusion | flops 3957800 | bytes 2683080 | tf_op jit(solution)/shard_map/reduce_sum | solution.py:139
  127.6 1.5 %fusion.7 = bf16[1,257,10,128]{3,1,2,0:T(8,128)(2,1)S(1)} fusion(f32[10,257]{1,0:T(8,128)S(1)} %get-tuple-element.7, f32[10,257]{1,0:T(8,128)S(1)} %bitcast.41, bf16[257,10,128]{2,1,0:T(8,128)(2,1)S(1)} %copy-done.8, f32[10,257,257]{1,2,0:T(8,128)S(1)} %copy-done.1, f32[10,257]{1,0:T(8,128)S(1)} %get-tuple-element.18), kind=kOutput, calls=%fused_computation.15 | convolution fusion | flops 172385312 | bytes 3988640 | tf_op jit(solution)/shard_map/bhij,bihd->bjhd/dot_general | solution.py:136
  129.1 2.1 %fusion.8 = bf16[1,257,10,128]{3,1,2,0:T(8,128)(2,1)S(1)} fusion(f32[10,257]{1,0:T(8,128)S(1)} %get-tuple-element.7, f32[10,257]{1,0:T(8,128)S(1)} %bitcast.42, bf16[257,10,128]{2,1,0:T(8,128)(2,1)S(1)} %copy-done.6, f32[10,257,257]{1,2,0:T(8,128)S(1)} %copy-done.1, f32[10,257]{1,0:T(8,128)S(1)} %get-tuple-element.18), kind=kOutput, calls=%fused_computation.16 | convolution fusion | flops 172385312 | bytes 3988640 | tf_op jit(solution)/shard_map/bhij,bjhd->bihd/dot_general | solution.py:132
  131.3 0.6 fusion.20
  131.9 1.2 convert_element_type.135
  133.2 0.2 copy.41
  133.3 1.2 convert_element_type.130
  134.6 0.2 copy.39
  134.8 1.2 convert_element_type.125
  136.0 0.9 fusion.33
  136.9 1.4 fusion.35
  (60 shorter events, 0.6 us)
Async XLA Ops:
  7.2 57.5 %all-gather.2.cloned.1.call-start = ((), (), s32[]{:S(2)}) async-start(), calls=%async_computation.2 | async-start | bytes 2949120 | tf_op jit(solution)/shard_map/all_gather | solution.py:66
  7.9 102.9 %reduce-scatter.3.cloned.1.call-start = ((), (), s32[]{:S(2)}) async-start(), calls=%async_computation.3 | async-start | bytes 163840 | tf_op jit(solution)/shard_map/reduce_scatter | solution.py:107
  9.4 4.5 %copy-start.7 = (bf16[257,10,128]{2,1,0:T(8,128)(2,1)}, bf16[257,10,128]{2,1,0:T(8,128)(2,1)S(1)}, u32[]{:S(2)}) copy-start(bf16[257,10,128]{2,1,0:T(8,128)(2,1)S(1)} %reshape.207) | copy-start | bytes 1973764
  11.2 2.7 %copy-start.5 = (bf16[257,10,128]{2,1,0:T(8,128)(2,1)}, bf16[257,10,128]{2,1,0:T(8,128)(2,1)S(1)}, u32[]{:S(2)}) copy-start(bf16[257,10,128]{2,1,0:T(8,128)(2,1)S(1)} %reshape.208) | copy-start | bytes 1973764
  13.0 4.0 %copy-start.3 = (bf16[257,10,128]{2,1,0:T(8,128)(2,1)}, bf16[257,10,128]{2,1,0:T(8,128)(2,1)S(1)}, u32[]{:S(2)}) copy-start(bf16[257,10,128]{2,1,0:T(8,128)(2,1)S(1)} %reshape.209) | copy-start | bytes 1973764
  17.0 1.9 %copy-start = (f32[10,257,257]{1,2,0:T(8,128)}, f32[10,257,257]{1,2,0:T(8,128)S(1)}, u32[]{:S(2)}) copy-start(f32[10,257,257]{1,2,0:T(8,128)S(1)} %get-tuple-element.19) | copy-start | bytes 7925884
  17.0 1.9 %copy-start.16 = (u32[32]{0:T(128)S(1)}, u32[32]{0:T(128)}, u32[]{:S(2)}) copy-start(u32[32]{0:T(128)} %constant.80) | copy-start | bytes 388
  17.0 2.5 %copy-start.12 = (u32[32]{0:T(128)S(1)}, u32[32]{0:T(128)}, u32[]{:S(2)}) copy-start(u32[32]{0:T(128)} %constant.85) | copy-start | bytes 388
  17.0 4.4 %copy-start.13 = (s32[8]{0:T(128)S(1)}, s32[8]{0:T(128)}, u32[]{:S(2)}) copy-start(s32[8]{0:T(128)} %param.17) | copy-start | bytes 100
  17.0 4.6 %copy-start.14 = (s32[8]{0:T(128)S(1)}, s32[8]{0:T(128)}, u32[]{:S(2)}) copy-start(s32[8]{0:T(128)} %param.19) | copy-start | bytes 100
  17.0 5.3 %copy-start.15 = (s32[8]{0:T(128)S(1)}, s32[8]{0:T(128)}, u32[]{:S(2)}) copy-start(s32[8]{0:T(128)} %param.18) | copy-start | bytes 100
  17.0 25.7 %copy-start.9 = (bf16[8,1024]{1,0:T(8,128)(2,1)S(1)}, bf16[8,1024]{1,0:T(8,128)(2,1)}, u32[]{:S(2)}) copy-start(bf16[8,1024]{1,0:T(8,128)(2,1)} %param.16) | copy-start | bytes 49156
  18.9 58.1 %copy-start.10 = (bf16[8,1024]{1,0:T(8,128)(2,1)S(1)}, bf16[8,1024]{1,0:T(8,128)(2,1)}, u32[]{:S(2)}) copy-start(bf16[8,1024]{1,0:T(8,128)(2,1)} %param.15) | copy-start | bytes 49156
  64.7 58.2 %copy-start.2 = (bf16[1280,1024]{1,0:T(8,128)(2,1)S(1)}, bf16[1280,1024]{1,0:T(8,128)(2,1)}, u32[]{:S(2)}) copy-start(bf16[1280,1024]{1,0:T(8,128)(2,1)} %all-gather.2.cloned.1.call-done) | copy-start | bytes 7864324
  91.6 44.4 %reduce-scatter.5.cloned.1.call-start = ((), (), s32[]{:S(2)}) async-start(), calls=%async_computation.4 | async-start | bytes 163840 | tf_op jit(solution)/shard_map/reduce_scatter | solution.py:108
  112.6 14.9 %copy-start.11 = (f32[8,1024]{1,0:T(8,128)}, f32[8,1024]{1,0:T(8,128)S(1)}, u32[]{:S(2)}) copy-start(f32[8,1024]{1,0:T(8,128)S(1)} %subtract_multiply_fusion) | copy-start | bytes 98308
  122.9 1.2 copy-start.4
  122.9 4.7 %copy-start.8 = (bf16[257,10,128]{2,1,0:T(8,128)(2,1)S(1)}, bf16[257,10,128]{2,1,0:T(8,128)(2,1)}, u32[]{:S(2)}) copy-start(bf16[257,10,128]{2,1,0:T(8,128)(2,1)} %copy-done.7) | copy-start | bytes 1973764
  123.7 3.9 %copy-start.1 = (f32[10,257,257]{1,2,0:T(8,128)S(1)}, f32[10,257,257]{1,2,0:T(8,128)}, u32[]{:S(2)}) copy-start(f32[10,257,257]{1,2,0:T(8,128)} %copy-done) | copy-start | bytes 7925884
  127.6 1.5 %copy-start.6 = (bf16[257,10,128]{2,1,0:T(8,128)(2,1)S(1)}, bf16[257,10,128]{2,1,0:T(8,128)(2,1)}, u32[]{:S(2)}) copy-start(bf16[257,10,128]{2,1,0:T(8,128)(2,1)} %copy-done.5) | copy-start | bytes 1973764
Sparse Core Ops, SparseCore 0:
  9.9 33.2 all-gather.1
  91.7 16.3 reduce-scatter.2
  110.5 17.4 reduce-scatter.4
where the time goes:
time: 146 us; the launch traced here: 145 us
  blocking collectives  90.6 us (62%)
  between operations  17.4 us (12%)
  local copies, waits for them, and re-layouts  13.3 us (9%)
  other arithmetic  11.5 us (8%)
  matrix products  11.3 us (8%)
    unnamed x3, blocking collectives  26.7 us
    all_gather x1, blocking collectives, on_device(): lax.all_gather(image_low, 'mp', axis=0, tiled=True)  13.1 us
    all_gather x1, blocking collectives, on_device(): lax.all_gather(text_low, 'mp', axis=0, tiled=True)  13.1 us
    psum x1, blocking collectives, broadcast(): return lax.psum(block, axis)  10.2 us
    psum x1, blocking collectives, on_device(): fresh = lax.psum(partial_value, 'mp')  10 us
    all_gather x1, blocking collectives, on_device(): piece_images = lax.all_gather(image_low, 'dp', axis=0, tiled=True)  8.86 us
    all_gather x1, blocking collectives, on_device(): piece_texts = lax.all_gather(text_low, 'dp', axis=0, tiled=True)  8.55 us
    unnamed x49, local copies, waits for them, and re-layouts  4.14 us
  transfers between devices with their start and end apart: 3, of which 0 were waited for; matrix products, arithmetic and copies ran while one was open for 20% of the time, Pallas kernels for 0%

commit v1 on v0

v1 whole, which is shorter than its diff:
```python
import functools
import math

import jax
import jax.numpy as jnp
from jax import lax
from jax.experimental import pallas as pl
from jax.experimental.pallas import tpu as pltpu
from jax.sharding import PartitionSpec as P

HEAD_DIM = 128
LOSS_SCALE = 8192.0
INV_ROOT = 1.0 / math.sqrt(HEAD_DIM)
F32 = jnp.float32
BF16 = jnp.bfloat16
LABEL_BASE = 64
DP_CHUNK = 8


def each_peer(count, body):
    if count <= 8:
        for k in range(1, count):
            body(k)
    else:
        lax.fori_loop(1, count, lambda k, c: (body(k), c)[1], 0)


def probs_t(queries, keys):
    scores = lax.dot_general(keys, queries, (((1,), (1,)), ((), ())), preferred_element_type=F32)
    scores = scores * INV_ROOT
    top = jnp.max(scores, axis=0, keepdims=True)
    grown = jnp.exp(scores - top)
    return grown * (1.0 / jnp.sum(grown, axis=0, keepdims=True))


def forward_kernel(
    n_dp, n_mp, heads, embed,
    q_ref, k_ref, v_ref, w_ref, img_ref, txt_ref, lab_ref, scale_ref, bias_ref,
    p_out, cot_out, igrad_out, tgrad_out, loss_out,
    pairs, probs, pooled, part, cols, fresh, sent, back,
    p_sem, za_s, za_r, xb_s, xb_r, cc_s, cc_r, e2_s, e2_r, e3_s, e3_r, e5_s, e5_r, e4_s, e4_r,
):
    dp = lax.axis_index("dp")
    mp = lax.axis_index("mp")
    n_q = n_dp // 2
    core = lax.rem(dp, 2)
    q_me = dp // 2
    sibling = dp + 1 - 2 * core
    rows = img_ref.shape[0]
    seq = q_ref.shape[1]
    cw = w_ref.shape[1]

    def dp_at(k):
        return lax.rem(dp + k, n_dp)

    def dp_from(k):
        return lax.rem(dp + n_dp - k, n_dp)

    def mp_at(k):
        return lax.rem(mp + k, n_mp)

    def mp_from(k):
        return lax.rem(mp + n_mp - k, n_mp)

    def chip_at(k):
        return 2 * lax.rem(q_me + k, n_q) + core

    def chip_from(k):
        return 2 * lax.rem(q_me + n_q - k, n_q) + core

    barrier = pltpu.get_barrier_semaphore()
    each_peer(n_mp, lambda k: pl.semaphore_signal(
        barrier, inc=1, device_id={"mp": mp_at(k)}, device_id_type=pl.DeviceIdType.MESH))
    each_peer(n_dp, lambda k: pl.semaphore_signal(
        barrier, inc=1, device_id={"dp": dp_at(k)}, device_id_type=pl.DeviceIdType.MESH))

    raw = jnp.concatenate([img_ref[...].astype(F32), txt_ref[...].astype(F32)], axis=0)
    norm = lax.rsqrt(jnp.sum(raw * raw, axis=1, keepdims=True) + 1e-06)
    pairs[dp, mp, :, :embed] = (raw * norm).astype(BF16)
    pairs[dp, mp, :, embed:] = lab_ref[...]
    pl.semaphore_wait(barrier, n_mp - 1 + n_dp - 1)

    def remote(src, dst, s_sem, r_sem, target):
        return pltpu.make_async_remote_copy(
            src_ref=src, dst_ref=dst, send_sem=s_sem, recv_sem=r_sem,
            device_id=target, device_id_type=pl.DeviceIdType.MESH)

    def za(k, slot):
        return remote(pairs.at[dp, slot], pairs.at[dp, slot], za_s.at[k], za_r.at[k], {"mp": mp_at(k)})

    def xb(k, block):
        return remote(pairs.at[block], pairs.at[block], xb_s.at[k], xb_r.at[k], {"dp": chip_at(k)})

    def cc(k, block):
        return remote(pairs.at[block], pairs.at[block], cc_s.at[k], cc_r.at[k], {"dp": sibling})

    each_peer(n_mp, lambda k: za(k, mp).start())

    def head(h):
        at = slice(h * HEAD_DIM, (h + 1) * HEAD_DIM)
        p = probs_t(q_ref[0, :, at], k_ref[0, :, at])
        probs[h] = p
        pltpu.make_async_copy(probs.at[h], p_out.at[h], p_sem.at[h]).start()
        mass = jnp.sum(p.astype(BF16).astype(F32), axis=1, keepdims=True)
        mean = jnp.sum(mass * v_ref[0, :, at].astype(F32), axis=0, keepdims=True) * (1.0 / seq)
        pooled[dp, :, at] = mean.astype(BF16).astype(F32)

    half = heads // 2
    for h in range(half):
        head(h)
    each_peer(n_mp, lambda k: za(k, mp_from(k)).wait_recv())
    each_peer(n_q, lambda k: xb(k, dp).start())
    cc(0, dp).start()
    for h in range(half, heads):
        head(h)

    def e2(k, slot):
        return remote(pooled.at[slot], pooled.at[slot], e2_s.at[k], e2_r.at[k], {"dp": dp_at(k)})

    each_peer(n_dp, lambda k: e2(k, dp).start())

    def relay(k):
        xb(k, chip_from(k)).wait_recv()
        cc(k, chip_from(k)).start()

    each_peer(n_q, relay)
    each_peer(n_dp, lambda k: e2(k, dp_from(k)).wait_recv())
    every = pooled[...].reshape(n_dp, heads * HEAD_DIM).astype(BF16)
    part[mp] = jnp.dot(every, w_ref[...], preferred_element_type=F32)

    def e3(k, slot):
        return remote(part.at[slot], part.at[slot], e3_s.at[k], e3_r.at[k], {"mp": mp_at(k)})

    each_peer(n_mp, lambda k: e3(k, mp).start())
    each_peer(n_mp, lambda k: e3(k, mp_from(k)).wait_recv())
    cols[dp] = jnp.sum(part[...], axis=0)

    def e5(k, slot):
        return remote(cols.at[slot], cols.at[slot], e5_s.at[k], e5_r.at[k], {"dp": dp_at(k)})

    each_peer(n_dp, lambda k: e5(k, dp).start())

    each_peer(n_mp, lambda k: za(k, mp).wait_send())
    each_peer(n_q, lambda k: xb(k, dp).wait_send())

    def settle(k):
        block = 2 * lax.rem(q_me + n_q - k, n_q) + core
        other = 2 * lax.rem(q_me + n_q - k, n_q) + 1 - core
        cc(k, block).wait_send()
        cc(k, other).wait_recv()

    settle(0)
    each_peer(n_q, settle)
    each_peer(n_dp, lambda k: e5(k, dp_from(k)).wait_recv())
    for c in range(n_dp):
        fresh[:, c * cw:(c + 1) * cw] = cols[c]

    raw_fresh = fresh[...]
    fresh_norm = lax.rsqrt(jnp.sum(raw_fresh * raw_fresh, axis=1, keepdims=True) + 1e-06)
    unit_fresh = raw_fresh * fresh_norm
    is_fresh = (lax.broadcasted_iota(jnp.int32, (2 * rows, 1), 0) == 0) & (mp == 0)
    raw = jnp.where(is_fresh, fresh[pl.ds(dp, 1), :], raw)
    norm = lax.rsqrt(jnp.sum(raw * raw, axis=1, keepdims=True) + 1e-06)
    unit = raw * norm

    fresh[...] = unit_fresh
    first = lax.broadcasted_iota(jnp.int32, (2 * rows, 1), 0) == 0

    def put_fresh(b):
        old = pairs[b, 0, :, :embed].astype(F32)
        pairs[b, 0, :, :embed] = jnp.where(first, fresh[pl.ds(b, 1), :], old).astype(BF16)

    put_fresh(0)
    each_peer(n_dp, put_fresh)

    units = jnp.concatenate([unit, unit_fresh], axis=0)
    norms = jnp.concatenate([norm, fresh_norm], axis=0)
    low = units.astype(BF16)
    count = units.shape[0]
    tags = pairs[:, 0, :, embed:].astype(F32)
    lead = lax.broadcasted_iota(jnp.int32, tags.shape, 1) == 0
    fresh_tags = jnp.sum(jnp.where(lead, tags, 0.0), axis=1)
    row_tags = jnp.concatenate([lab_ref[...].astype(F32), fresh_tags], axis=0)
    row_a = row_tags[:, 0:1] * LABEL_BASE + row_tags[:, 1:2]
    row_b = row_tags[:, 2:3] * LABEL_BASE + row_tags[:, 3:4]
    row_spot = lax.broadcasted_iota(jnp.int32, (count, 1), 0)
    row_text = (row_spot >= rows) & (row_spot < 2 * rows)
    temper = jnp.exp(jnp.full((1, 1), scale_ref[0], F32))
    offset = bias_ref[0]

    step = min(DP_CHUNK, n_dp)
    wide = step * n_mp * 2 * rows

    def chunk(at):
        block = pairs[pl.ds(at * step, step), :, :, :embed].reshape(wide, embed)
        col_tags = pairs[pl.ds(at * step, step), :, :, embed:].reshape(wide, 128).astype(F32).T
        col_a = col_tags[0:1, :] * LABEL_BASE + col_tags[1:2, :]
        col_b = col_tags[2:3, :] * LABEL_BASE + col_tags[3:4, :]
        spot = lax.broadcasted_iota(jnp.int32, (1, wide), 1)
        col_text = lax.rem(spot, 2 * rows) >= rows
        valid = row_text != col_text
        scores = lax.dot_general(low, block, (((1,), (1,)), ((), ())), preferred_element_type=F32)
        logits = temper * scores + offset
        signed = jnp.where((row_a == col_a) | (row_b == col_b), 1.0, -1.0)
        margin = signed * logits
        tail = jnp.exp(-jnp.abs(margin))
        log_sig = jnp.minimum(margin, 0.0) - jnp.log1p(tail)
        losses = -jnp.sum(jnp.where(valid, log_sig, 0.0), axis=1, keepdims=True)
        against = jnp.where(margin >= 0, tail, 1.0) / (1.0 + tail)
        coeffs = jnp.where(valid, temper * (-signed * against), 0.0).astype(BF16)
        return jnp.dot(coeffs, block, preferred_element_type=F32), losses

    if n_dp == step:
        direction, losses = chunk(0)
    else:
        def more(at, carry):
            new = chunk(at)
            return carry[0] + new[0], carry[1] + new[1]
        direction, losses = lax.fori_loop(
            0, n_dp // step, more, (jnp.zeros((count, embed), F32), jnp.zeros((count, 1), F32)))

    grads = (direction - units * jnp.sum(units * direction, axis=1, keepdims=True)) * norms
    fresh_low = grads[2 * rows:].astype(BF16)

    if cw % 128 == 0:
        fresh[...] = fresh_low.astype(F32)
        mine = fresh[:, pl.ds(pl.multiple_of(dp * cw, 128), cw)].astype(BF16)
    else:
        spot = lax.broadcasted_iota(jnp.int32, (embed, cw), 0)
        want = lax.broadcasted_iota(jnp.int32, (embed, cw), 1) + dp * cw
        pick = jnp.where(spot == want, 1.0, 0.0).astype(BF16)
        mine = jnp.dot(fresh_low, pick, preferred_element_type=F32).astype(BF16)
    spread = lax.dot_general(mine, w_ref[...], (((1,), (1,)), ((), ())), preferred_element_type=F32)
    for b in range(n_dp):
        sent[b] = spread[b:b + 1, :]
    back[dp] = sent[dp]

    def e4(k, src, dst):
        return remote(sent.at[src], back.at[dst], e4_s.at[k], e4_r.at[k], {"dp": dp_at(k)})

    each_peer(n_dp, lambda k: e4(k, dp_at(k), dp).start())

    igrad_out[...] = grads[:rows]
    tgrad_out[...] = grads[rows:2 * rows]
    loss_out[...] = jnp.broadcast_to(losses[:rows], loss_out.shape)
    for h in range(heads):
        pltpu.make_async_copy(probs.at[h], p_out.at[h], p_sem.at[h]).wait()
    each_peer(n_dp, lambda k: e2(k, dp).wait_send())
    each_peer(n_mp, lambda k: e3(k, mp).wait_send())
    each_peer(n_dp, lambda k: e5(k, dp).wait_send())
    each_peer(n_dp, lambda k: e4(k, dp_at(k), dp_from(k)).wait_recv())
    total = jnp.sum(back[...], axis=0)
    cot_out[...] = (total * (LOSS_SCALE / seq)).astype(BF16).astype(F32)
    each_peer(n_dp, lambda k: e4(k, dp_at(k), dp).wait_send())


def backward_kernel(q_ref, k_ref, v_ref, p_ref, cot_ref, qg_ref, kg_ref, vg_ref):
    p = p_ref[0]
    cot = cot_ref[...]
    prob_grad = jnp.sum(v_ref[0].astype(F32) * cot, axis=1, keepdims=True)
    centre = jnp.sum(p * prob_grad, axis=0, keepdims=True)
    score_grad = (p * (prob_grad - centre)).astype(BF16)
    qg_ref[0] = (lax.dot_general(
        score_grad, k_ref[0], (((0,), (0,)), ((), ())), preferred_element_type=F32
    ) * INV_ROOT).astype(BF16)
    kg_ref[0] = (jnp.dot(score_grad, q_ref[0], preferred_element_type=F32) * INV_ROOT).astype(BF16)
    mass = jnp.sum(p.astype(BF16).astype(F32), axis=1, keepdims=True)
    vg_ref[0] = (mass * cot).astype(BF16)


def on_device(
    n_dp, n_mp,
    query_tokens, key_tokens, value_tokens, head_weight, image_cache, text_embed,
    text_pair, image_group, text_group, logit_scale, logit_bias,
):
    _, seq, width = query_tokens.shape
    heads = width // HEAD_DIM
    rows, embed = image_cache.shape
    cw = head_weight.shape[1]
    dp = lax.axis_index("dp")
    mp = lax.axis_index("mp")
    index = (dp * n_mp + mp) * rows + jnp.arange(rows, dtype=jnp.int32)
    first = jnp.concatenate([index, text_pair])
    second = jnp.concatenate([image_group, text_group])
    lane = jnp.arange(128, dtype=jnp.int32)[None, :]
    first, second = first[:, None], second[:, None]
    labels = jnp.where(
        lane == 0, first // LABEL_BASE,
        jnp.where(lane == 1, first % LABEL_BASE,
                  jnp.where(lane == 2, second // LABEL_BASE, second % LABEL_BASE)),
    ).astype(BF16)

    vmem = pl.BlockSpec(memory_space=pltpu.VMEM)
    smem = pl.BlockSpec(memory_space=pltpu.SMEM)
    n_q = n_dp // 2
    dma = pltpu.SemaphoreType.DMA
    probs, cot, image_grad, text_grad, loss = pl.pallas_call(
        functools.partial(forward_kernel, n_dp, n_mp, heads, embed),
        out_shape=(
            jax.ShapeDtypeStruct((heads, seq, seq), F32),
            jax.ShapeDtypeStruct((1, width), F32),
            jax.ShapeDtypeStruct((rows, embed), F32),
            jax.ShapeDtypeStruct((rows, embed), F32),
            jax.ShapeDtypeStruct((rows, 128), F32),
        ),
        in_specs=[vmem] * 7 + [smem] * 2,
        out_specs=(pl.BlockSpec(memory_space=pl.ANY), vmem, vmem, vmem, vmem),
        scratch_shapes=[
            pltpu.VMEM((n_dp, n_mp, 2 * rows, embed + 128), BF16),
            pltpu.VMEM((heads, seq, seq), F32),
            pltpu.VMEM((n_dp, 1, width), F32),
            pltpu.VMEM((n_mp, n_dp, cw), F32),
            pltpu.VMEM((n_dp, n_dp, cw), F32),
            pltpu.VMEM((n_dp, embed), F32),
            pltpu.VMEM((n_dp, 1, width), F32),
            pltpu.VMEM((n_dp, 1, width), F32),
            dma((heads,)),
            dma((n_mp,)), dma((n_mp,)),
            dma((n_q,)), dma((n_q,)),
            dma((n_q,)), dma((n_q,)),
            dma((n_dp,)), dma((n_dp,)),
            dma((n_mp,)), dma((n_mp,)),
            dma((n_dp,)), dma((n_dp,)),
            dma((n_dp,)), dma((n_dp,)),
        ],
        compiler_params=pltpu.CompilerParams(
            collective_id=0, has_side_effects=True, vmem_limit_bytes=56 * 2**20),
        name="forward_pairs",
    )(
        query_tokens, key_tokens, value_tokens, head_weight, image_cache, text_embed,
        labels, logit_scale.reshape(1), logit_bias.reshape(1),
    )

    token = pl.BlockSpec((1, seq, HEAD_DIM), lambda h: (0, 0, h))
    query_grad, key_grad, value_grad = pl.pallas_call(
        backward_kernel,
        grid=(heads,),
        out_shape=(jax.ShapeDtypeStruct(query_tokens.shape, BF16),) * 3,
        in_specs=[
            token, token, token,
            pl.BlockSpec((1, seq, seq), lambda h: (h, 0, 0)),
            pl.BlockSpec((1, HEAD_DIM), lambda h: (0, h)),
        ],
        out_specs=(token, token, token),
        name="attention_back",
    )(query_tokens, key_tokens, value_tokens, probs, cot)
    return query_grad, key_grad, value_grad, image_grad, text_grad, loss[:, 0]


def solution(mesh):
    pair_rows = P(("dp", "mp"), None)
    pair = P(("dp", "mp"))
    tokens = P("dp", None, "mp")
    return jax.shard_map(
        functools.partial(on_device, mesh.shape["dp"], mesh.shape["mp"]),
        mesh=mesh,
        in_specs=(
            tokens, tokens, tokens, P("mp", "dp"), pair_rows, pair_rows, pair, pair, pair, P(), P(),
        ),
        out_specs=(tokens, tokens, tokens, pair_rows, pair_rows, pair),
        check_vma=False,
    )
```

time: 146 us -> 48 us (0.33)
  blocking collectives: 90.6 us -> 0 us
  Pallas kernels: 0 us -> 41.6 us
  between operations: 17.4 us -> 1.99 us
  local copies, waits for them, and re-layouts: 13.3 us -> 1.87 us
  matrix products: 11.3 us -> 0 us
  other arithmetic: 11.5 us -> 2.18 us
    all_gather x4 -> x0, blocking collectives: 43.7 us -> none  [the longest x1 13.1 us: on_device(): lax.all_gather(image_low, 'mp', axis=0, tiled=True)]
    pallas_call x0 -> x2, Pallas kernels: none -> 41.6 us  [the longest x1 32.5 us: on_device(): pl.pallas_call(functools.partial(forward_kernel, n_dp, n_mp, heads, embed...]
    unnamed x3 -> x0, blocking collectives: 26.7 us -> none
    psum x2 -> x0, blocking collectives: 20.2 us -> none  [the longest x1 10.2 us: broadcast(): return lax.psum(block, axis)]
    dot_general x10 -> x0, matrix products: 11.3 us -> none  [the longest x1 2.34 us: on_device(): jnp.dot(pooled, full_weight, preferred_element_type=jnp.float32)]
    reduce_sum x5 -> x0, other arithmetic: 5.34 us -> none  [the longest x1 3.13 us: on_device(): column_mass = jnp.sum(probs_low, axis=2, dtype=jnp.float32)]
    convert_element_type x6 -> x0, local copies, waits for them, and re-layouts: 4.07 us -> none  [the longest x2 1.41 us: on_device(): key_grad.reshape(out_shape).astype(jnp.bfloat16)]
    another operation x2 -> x0, local copies, waits for them, and re-layouts: 3.54 us -> none
  transfers between devices with their start and end apart: 3 -> 0, of which waited for: 0 -> 0; matrix products, arithmetic and copies ran while one was open for 20% -> 0% of each run, Pallas kernels for 0% -> 0%
where the time goes in v1:
time: 48 us; the launch traced here: 47.7 us
  Pallas kernels  41.6 us (87%)
  other arithmetic  2.18 us (5%)
  between operations  1.99 us (4%)
  local copies, waits for them, and re-layouts  1.87 us (4%)
    pallas_call x1, Pallas kernels, on_device(): pl.pallas_call(functools.partial(forward_kernel, n_dp, n_mp, heads, embed...  32.5 us
    pallas_call x1, Pallas kernels, on_device(): pl.pallas_call(backward_kernel, grid=(heads,), out_shape=(jax.ShapeDtypeS...  9.1 us
    unnamed x8, local copies, waits for them, and re-layouts  1.24 us

profile of v1, /device:TPU:0, one launch (start us, length us, event | category | flops | bytes accessed | tf_op | source)
XLA Modules:
  0.0 47.7 jit_solution(4762609299544142022)
XLA Ops:
  2.0 0.7 %and_select_fusion.3 = (s32[16]{0:T(128)S(1)}, s32[16]{0:T(128)S(1)}) fusion(s32[8]{0:T(128)} %param.17, s32[8]{0:T(128)S(1)} %iota_add_fusion), kind=kLoop, calls=%fused_computation.5 | loop fusion | flops 256 | bytes 192 | tf_op jit(solution)/shard_map/jit(floor_divide)/jit(_where)/select_n | solution.py:288
  2.7 0.8 %and_select_fusion.1 = (s32[16]{0:T(128)S(1)}, s32[16]{0:T(128)S(1)}) fusion(s32[8]{0:T(128)} %param.19, s32[8]{0:T(128)} %param.18), kind=kLoop, calls=%fused_computation.3 | loop fusion | flops 256 | bytes 192 | tf_op jit(solution)/shard_map/jit(floor_divide)/jit(_where)/select_n | solution.py:290
  3.5 0.7 %select_convert_fusion.lab_ref = bf16[16,128]{1,0:T(8,128)(2,1)} fusion(s32[16]{0:T(128)S(1)} %get-tuple-element.26, s32[16]{0:T(128)S(1)} %get-tuple-element.24, s32[16]{0:T(128)S(1)} %get-tuple-element.27, s32[16]{0:T(128)S(1)} %get-tuple-element.22, pred[128]{0:T(512)(128)(4,1)S(1)} %get-tuple-element.28, pred[128]{0:T(512)(128)(4,1)S(1)} %get-tuple-element.29, ...), kind=kLoop, calls=%fused_computation | loop fusion | flops 8192 | bytes 4736 | tf_op jit(solution)/shard_map/convert_element_type | solution.py:291
  4.1 32.5 %forward_pairs.1 = (f32[10,257,257]{2,1,0:T(8,128)}, f32[1,1280]{1,0:T(1,128)}, f32[8,1024]{1,0:T(8,128)}, f32[8,1024]{1,0:T(8,128)}, f32[8,128]{1,0:T(8,128)}) custom-call(bf16[1,257,1280]{2,1,0:T(8,128)(2,1)} %q_ref.3, bf16[1,257,1280]{2,1,0:T(8,128)(2,1)} %k_ref.3, bf16[1,257,1280]{2,1,0:T(8,128)(2,1)} %v_ref.3, bf16[1280,128]{1,0:T(8,128)(2,1)} %w_ref.1, ...), custom_call_target="tpu_custom_call" | custom-call | tf_op jit(solution)/shard_map/forward_pairs/pallas_call | solution.py:297
  36.7 0.0 copy-start.2
  36.7 0.0 copy-start.1
  36.7 0.0 copy-start
  36.7 9.1 %attention_back.1 = (bf16[1,257,1280]{2,1,0:T(8,128)(2,1)}, bf16[1,257,1280]{2,1,0:T(8,128)(2,1)}, bf16[1,257,1280]{2,1,0:T(8,128)(2,1)}) custom-call(bf16[1,257,1280]{2,1,0:T(8,128)(2,1)} %q_ref.3, bf16[1,257,1280]{2,1,0:T(8,128)(2,1)} %k_ref.3, bf16[1,257,1280]{2,1,0:T(8,128)(2,1)} %v_ref.3, f32[10,257,257]{2,1,0:T(8,128)} %get-tuple-element.14.p_ref, ...), custom_call_target="tpu_custom_call" | custom-call | tf_op jit(solution)/shard_map/attention_back/pallas_call | solution.py:335
  45.8 0.0 copy-done.2
  45.8 0.6 %slice_reduce_fusion = f32[8]{0:T(128)} fusion(f32[8,128]{1,0:T(8,128)S(1)} %copy-done.2), kind=kLoop, calls=%fused_computation.1 | loop fusion | bytes 64 | tf_op jit(solution)/shard_map/slice | solution.py:347
  46.4 0.0 copy-done.1
  46.4 0.6 %copy.21 = f32[8,1024]{1,0:T(8,128)} copy(f32[8,1024]{1,0:T(8,128)S(1)} %copy-done.1) | data formatting | bytes 65536
  47.0 0.0 copy-done
  47.1 0.6 %copy.22 = f32[8,1024]{1,0:T(8,128)} copy(f32[8,1024]{1,0:T(8,128)S(1)} %copy-done) | data formatting | bytes 65536
  (4 shorter events, 0.0 us)
Async XLA Ops:
  36.7 9.1 %copy-start.2 = (f32[8,128]{1,0:T(8,128)S(1)}, f32[8,128]{1,0:T(8,128)}, u32[]{:S(2)}) copy-start(f32[8,128]{1,0:T(8,128)} %get-tuple-element.21) | copy-start | bytes 12292
  36.7 9.8 %copy-start.1 = (f32[8,1024]{1,0:T(8,128)S(1)}, f32[8,1024]{1,0:T(8,128)}, u32[]{:S(2)}) copy-start(f32[8,1024]{1,0:T(8,128)} %get-tuple-element.39) | copy-start | bytes 98308
  36.7 10.4 %copy-start = (f32[8,1024]{1,0:T(8,128)S(1)}, f32[8,1024]{1,0:T(8,128)}, u32[]{:S(2)}) copy-start(f32[8,1024]{1,0:T(8,128)} %get-tuple-element.40) | copy-start | bytes 98308

commit v2 on v1

v2 whole, which is shorter than its diff:
```python
import functools
import math

import jax
import jax.numpy as jnp
from jax import lax
from jax.experimental import pallas as pl
from jax.experimental.pallas import tpu as pltpu
from jax.sharding import PartitionSpec as P

HEAD_DIM = 128
LOSS_SCALE = 8192.0
INV_ROOT = 1.0 / math.sqrt(HEAD_DIM)
F32 = jnp.float32
BF16 = jnp.bfloat16
LABEL_BASE = 64
LOG2_E = 1.0 / math.log(2.0)
DP_CHUNK = 8


def each_peer(count, body):
    if count <= 8:
        for k in range(1, count):
            body(k)
    else:
        lax.fori_loop(1, count, lambda k, c: (body(k), c)[1], 0)


def probs_t(queries, keys):
    scores = lax.dot_general(keys, queries, (((1,), (1,)), ((), ())), preferred_element_type=F32)
    top = jnp.max(scores, axis=0, keepdims=True)
    grown = jnp.exp2((scores - top) * (INV_ROOT * LOG2_E))
    return grown * (1.0 / jnp.sum(grown, axis=0, keepdims=True))


def column_mass(probs_low):
    ones = jnp.ones((probs_low.shape[1], HEAD_DIM), BF16)
    return jnp.dot(probs_low, ones, preferred_element_type=F32)


def pair_terms(scores, same, valid, temper, offset):
    logits = temper * scores + offset
    signed = jnp.where(same, 1.0, -1.0)
    margin = signed * logits
    tail = jnp.exp(-jnp.abs(margin))
    log_sig = jnp.minimum(margin, 0.0) - jnp.log1p(tail)
    against = jnp.where(margin >= 0, tail, 1.0) / (1.0 + tail)
    coeffs = temper * (-signed * against)
    if valid is not None:
        log_sig = jnp.where(valid, log_sig, 0.0)
        coeffs = jnp.where(valid, coeffs, 0.0)
    return coeffs.astype(BF16), -jnp.sum(log_sig, axis=1, keepdims=True)


def row_labels(tags):
    return tags[:, 0:1] * LABEL_BASE + tags[:, 1:2], tags[:, 2:3] * LABEL_BASE + tags[:, 3:4]


def lane_labels(tags):
    turned = tags.T
    return (turned[0:1, :] * LABEL_BASE + turned[1:2, :],
            turned[2:3, :] * LABEL_BASE + turned[3:4, :])


def nt_dot(left, right):
    return lax.dot_general(left, right, (((1,), (1,)), ((), ())), preferred_element_type=F32)


def forward_kernel(
    n_dp, n_mp, heads, embed,
    q_in, k_in, v_in, w_in, img_ref, txt_ref, tpair_ref, igroup_ref, tgroup_ref, scale_ref, bias_ref,
    p_out, cot_out, igrad_out, tgrad_out, loss_out,
    q_ref, k_ref, v_ref, w_ref, pairs, texts, probs, pooled, part, cols, fresh, sent, back,
    in_sem, p_sem, za_s, za_r, xb_s, xb_r, cc_s, cc_r, e2_s, e2_r, e3_s, e3_r, e5_s, e5_r, e4_s, e4_r,
):
    dp = lax.axis_index("dp")
    mp = lax.axis_index("mp")
    n_q = n_dp // 2
    core = lax.rem(dp, 2)
    q_me = dp // 2
    sibling = dp + 1 - 2 * core
    rows = img_ref.shape[0]
    seq = q_ref.shape[1]
    cw = w_ref.shape[1]

    def dp_at(k):
        return lax.rem(dp + k, n_dp)

    def dp_from(k):
        return lax.rem(dp + n_dp - k, n_dp)

    def mp_at(k):
        return lax.rem(mp + k, n_mp)

    def mp_from(k):
        return lax.rem(mp + n_mp - k, n_mp)

    def chip_at(k):
        return 2 * lax.rem(q_me + k, n_q) + core

    def chip_from(k):
        return 2 * lax.rem(q_me + n_q - k, n_q) + core

    loads = [
        pltpu.make_async_copy(src, dst, in_sem.at[i])
        for i, (src, dst) in enumerate(
            ((q_in, q_ref), (k_in, k_ref), (v_in, v_ref), (w_in, w_ref)))
    ]
    for load in loads:
        load.start()
    barrier = pltpu.get_barrier_semaphore()
    each_peer(n_mp, lambda k: pl.semaphore_signal(
        barrier, inc=1, device_id={"mp": mp_at(k)}, device_id_type=pl.DeviceIdType.MESH))
    each_peer(n_dp, lambda k: pl.semaphore_signal(
        barrier, inc=1, device_id={"dp": dp_at(k)}, device_id_type=pl.DeviceIdType.MESH))

    raw = jnp.concatenate([img_ref[...].astype(F32), txt_ref[...].astype(F32)], axis=0)
    norm = lax.rsqrt(jnp.sum(raw * raw, axis=1, keepdims=True) + 1e-06)
    pairs[dp, mp, :, :embed] = (raw * norm).astype(BF16)
    spot = lax.broadcasted_iota(jnp.int32, (2 * rows, 128), 0)
    lane = lax.broadcasted_iota(jnp.int32, (2 * rows, 128), 1)
    first = (dp * n_mp + mp) * rows + spot
    second = jnp.zeros_like(spot)
    for r in range(rows):
        first = jnp.where(spot == rows + r, tpair_ref[r], first)
        second = jnp.where(spot == r, igroup_ref[r], second)
        second = jnp.where(spot == rows + r, tgroup_ref[r], second)
    label = jnp.where(lane < 2, first, second)
    own_tags = jnp.where(lax.rem(lane, 2) == 0, label // LABEL_BASE, lax.rem(label, LABEL_BASE))
    own_tags = own_tags.astype(F32)
    pairs[dp, mp, :, embed:] = own_tags.astype(BF16)
    pl.semaphore_wait(barrier, n_mp - 1 + n_dp - 1)

    def remote(src, dst, s_sem, r_sem, target):
        return pltpu.make_async_remote_copy(
            src_ref=src, dst_ref=dst, send_sem=s_sem, recv_sem=r_sem,
            device_id=target, device_id_type=pl.DeviceIdType.MESH)

    def za(k, slot):
        return remote(pairs.at[dp, slot], pairs.at[dp, slot], za_s.at[k], za_r.at[k], {"mp": mp_at(k)})

    def xb(k, block):
        return remote(pairs.at[block], pairs.at[block], xb_s.at[k], xb_r.at[k], {"dp": chip_at(k)})

    def cc(k, block):
        return remote(pairs.at[block], pairs.at[block], cc_s.at[k], cc_r.at[k], {"dp": sibling})

    each_peer(n_mp, lambda k: za(k, mp).start())

    for load in loads[:3]:
        load.wait()

    def head(h):
        at = slice(h * HEAD_DIM, (h + 1) * HEAD_DIM)
        p = probs_t(q_ref[0, :, at], k_ref[0, :, at])
        probs[h] = p
        mass = column_mass(p.astype(BF16))
        mean = jnp.sum(mass * v_ref[0, :, at].astype(F32), axis=0, keepdims=True) * (1.0 / seq)
        pooled[dp, :, at] = mean.astype(BF16).astype(F32)

    def keep(h):
        return pltpu.make_async_copy(probs.at[h], p_out.at[h], p_sem.at[h])

    early = 2 * heads // 5
    for h in range(early):
        head(h)
    each_peer(n_mp, lambda k: za(k, mp_from(k)).wait_recv())
    each_peer(n_q, lambda k: xb(k, dp).start())
    cc(0, dp).start()
    for h in range(early, heads):
        head(h)

    def e2(k, slot):
        return remote(pooled.at[slot], pooled.at[slot], e2_s.at[k], e2_r.at[k], {"dp": dp_at(k)})

    each_peer(n_dp, lambda k: e2(k, dp).start())

    for h in range(heads):
        keep(h).start()
    loads[3].wait()
    each_peer(n_dp, lambda k: e2(k, dp_from(k)).wait_recv())
    every = pooled[...].reshape(n_dp, heads * HEAD_DIM).astype(BF16)
    part[mp] = jnp.dot(every, w_ref[...], preferred_element_type=F32)

    def e3(k, slot):
        return remote(part.at[slot], part.at[slot], e3_s.at[k], e3_r.at[k], {"mp": mp_at(k)})

    each_peer(n_mp, lambda k: e3(k, mp).start())

    def relay(k):
        xb(k, chip_from(k)).wait_recv()
        cc(k, chip_from(k)).start()

    each_peer(n_q, relay)
    each_peer(n_mp, lambda k: e3(k, mp_from(k)).wait_recv())
    cols[dp] = jnp.sum(part[...], axis=0)

    def e5(k, slot):
        return remote(cols.at[slot], cols.at[slot], e5_s.at[k], e5_r.at[k], {"dp": dp_at(k)})

    each_peer(n_dp, lambda k: e5(k, dp).start())

    def settle(k):
        block = 2 * lax.rem(q_me + n_q - k, n_q) + 1 - core
        cc(k, block).wait_recv()

    settle(0)
    each_peer(n_q, settle)

    unit = raw * norm
    low = unit.astype(BF16)
    temper = jnp.exp(jnp.full((1, 1), scale_ref[0], F32))
    offset = bias_ref[0]
    own_a, own_b = row_labels(own_tags)
    own_text = lax.broadcasted_iota(jnp.int32, (2 * rows, 1), 0) >= rows
    step = min(DP_CHUNK, n_dp)
    wide = step * n_mp * 2 * rows

    def chunk(at):
        block = pairs[pl.ds(at * step, step), :, :, :embed].reshape(wide, embed)
        col_a, col_b = lane_labels(
            pairs[pl.ds(at * step, step), :, :, embed:].reshape(wide, 128).astype(F32))
        spot = lax.broadcasted_iota(jnp.int32, (1, wide), 1)
        col_text = lax.rem(spot, 2 * rows) >= rows
        valid = (own_text != col_text) & (lax.rem(spot, n_mp * 2 * rows) != 0)
        same = (own_a == col_a) | (own_b == col_b)
        coeffs, losses = pair_terms(nt_dot(low, block), same, valid, temper, offset)
        return jnp.dot(coeffs, block, preferred_element_type=F32), losses

    if n_dp == step:
        direction, losses = chunk(0)
    else:
        def more(at, carry):
            new = chunk(at)
            return carry[0] + new[0], carry[1] + new[1]
        direction, losses = lax.fori_loop(
            0, n_dp // step, more,
            (jnp.zeros((2 * rows, embed), F32), jnp.zeros((2 * rows, 1), F32)))

    def copy_texts(b):
        texts[b] = pairs[b, :, :, :embed].astype(F32)[:, rows:].reshape(
            n_mp * rows, embed).astype(BF16)

    copy_texts(0)
    each_peer(n_dp, copy_texts)
    text_a, text_b = lane_labels(
        pairs[:, :, :, embed:].astype(F32)[:, :, rows:].reshape(n_dp * n_mp * rows, 128))
    tags = pairs[:, 0, :, embed:].astype(F32)
    lead = lax.broadcasted_iota(jnp.int32, tags.shape, 1) == 0
    fresh_tags = jnp.sum(jnp.where(lead, tags, 0.0), axis=1)
    fresh_a, fresh_b = row_labels(fresh_tags)
    fresh_lane_a, fresh_lane_b = lane_labels(fresh_tags)
    fresh_same = (fresh_a == text_a) | (fresh_b == text_b)
    back_same = (own_a[rows:] == fresh_lane_a) | (own_b[rows:] == fresh_lane_b)
    all_texts = texts[...].reshape(n_dp * n_mp * rows, embed)

    each_peer(n_dp, lambda k: e5(k, dp_from(k)).wait_recv())
    for c in range(n_dp):
        fresh[:, c * cw:(c + 1) * cw] = cols[c]
    raw_fresh = fresh[...]
    fresh_norm = lax.rsqrt(jnp.sum(raw_fresh * raw_fresh, axis=1, keepdims=True) + 1e-06)
    unit_fresh = raw_fresh * fresh_norm
    low_fresh = unit_fresh.astype(BF16)
    coeffs, fresh_loss = pair_terms(
        nt_dot(low_fresh, all_texts), fresh_same, None, temper, offset)
    fresh_dir = jnp.dot(coeffs, all_texts, preferred_element_type=F32)
    fresh_grad = (
        fresh_dir - unit_fresh * jnp.sum(unit_fresh * fresh_dir, axis=1, keepdims=True)
    ) * fresh_norm
    fresh_low = fresh_grad.astype(BF16)

    if cw % 128 == 0:
        fresh[...] = fresh_low.astype(F32)
        mine = fresh[:, pl.ds(pl.multiple_of(dp * cw, 128), cw)].astype(BF16)
    else:
        spot = lax.broadcasted_iota(jnp.int32, (embed, cw), 0)
        want = lax.broadcasted_iota(jnp.int32, (embed, cw), 1) + dp * cw
        pick = jnp.where(spot == want, 1.0, 0.0).astype(BF16)
        mine = jnp.dot(fresh_low, pick, preferred_element_type=F32).astype(BF16)
    spread = lax.dot_general(mine, w_ref[...], (((1,), (1,)), ((), ())), preferred_element_type=F32)
    for b in range(n_dp):
        sent[b] = spread[b:b + 1, :]
    back[dp] = sent[dp]

    def e4(k, src, dst):
        return remote(sent.at[src], back.at[dst], e4_s.at[k], e4_r.at[k], {"dp": dp_at(k)})

    each_peer(n_dp, lambda k: e4(k, dp_at(k), dp).start())

    coeffs, unused = pair_terms(
        nt_dot(low[rows:], low_fresh), back_same, None, temper, offset)
    added = jnp.dot(coeffs, low_fresh, preferred_element_type=F32)
    text_dir = direction[rows:] + added
    unit_text = unit[rows:]
    tgrad_out[...] = (
        text_dir - unit_text * jnp.sum(unit_text * text_dir, axis=1, keepdims=True)
    ) * norm[rows:]
    unit_image, image_dir = unit[:rows], direction[:rows]
    image_grad = (
        image_dir - unit_image * jnp.sum(unit_image * image_dir, axis=1, keepdims=True)
    ) * norm[:rows]
    is_fresh = (lax.broadcasted_iota(jnp.int32, (rows, 1), 0) == 0) & (mp == 0)
    fresh[...] = fresh_grad
    igrad_out[...] = jnp.where(is_fresh, fresh[pl.ds(dp, 1), :], image_grad)
    is_mine = lax.broadcasted_iota(jnp.int32, (n_dp, 1), 0) == dp
    my_loss = jnp.sum(jnp.where(is_mine, fresh_loss, 0.0), axis=0, keepdims=True)
    row_loss = jnp.where(is_fresh, my_loss, losses[:rows])
    loss_out[...] = jnp.broadcast_to(row_loss, (rows, 128)).T[0:1, :]

    for h in range(heads):
        keep(h).wait()
    each_peer(n_mp, lambda k: za(k, mp).wait_send())
    each_peer(n_q, lambda k: xb(k, dp).wait_send())
    cc(0, dp).wait_send()
    each_peer(n_q, lambda k: cc(k, chip_from(k)).wait_send())
    each_peer(n_dp, lambda k: e2(k, dp).wait_send())
    each_peer(n_mp, lambda k: e3(k, mp).wait_send())
    each_peer(n_dp, lambda k: e5(k, dp).wait_send())
    each_peer(n_dp, lambda k: e4(k, dp_at(k), dp_from(k)).wait_recv())
    total = jnp.sum(back[...], axis=0)
    cot_out[...] = (total * (LOSS_SCALE / seq)).astype(BF16).astype(F32)
    each_peer(n_dp, lambda k: e4(k, dp_at(k), dp).wait_send())


def backward_kernel(
    group, seq,
    q_ref, k_ref, v_ref, p_ref, cot_ref, igrad_ref, tgrad_ref, loss_ref,
    qg_ref, kg_ref, vg_ref, igrad_out, tgrad_out, loss_out,
):
    @pl.when(pl.program_id(0) == 0)
    def _():
        igrad_out[...] = igrad_ref[...]
        tgrad_out[...] = tgrad_ref[...]
        loss_out[...] = loss_ref[...]

    for h in range(group):
        at = slice(h * HEAD_DIM, (h + 1) * HEAD_DIM)
        p = p_ref[h]
        cot = cot_ref[:, at]
        repeated = jnp.broadcast_to(cot, (HEAD_DIM, HEAD_DIM)).astype(BF16)
        prob_grad = nt_dot(v_ref[0, :, at], repeated)
        prob_grad = jnp.concatenate([prob_grad] * pl.cdiv(seq, HEAD_DIM), axis=1)[:, :seq]
        centre = jnp.sum(p * prob_grad, axis=0, keepdims=True)
        score_grad = (p * (prob_grad - centre)).astype(BF16)
        qg_ref[0, :, at] = (lax.dot_general(
            score_grad, k_ref[0, :, at], (((0,), (0,)), ((), ())), preferred_element_type=F32
        ) * INV_ROOT).astype(BF16)
        kg_ref[0, :, at] = (jnp.dot(
            score_grad, q_ref[0, :, at], preferred_element_type=F32
        ) * INV_ROOT).astype(BF16)
        vg_ref[0, :, at] = (column_mass(p.astype(BF16)) * cot).astype(BF16)


def on_device(
    n_dp, n_mp,
    query_tokens, key_tokens, value_tokens, head_weight, image_cache, text_embed,
    text_pair, image_group, text_group, logit_scale, logit_bias,
):
    _, seq, width = query_tokens.shape
    heads = width // HEAD_DIM
    rows, embed = image_cache.shape
    cw = head_weight.shape[1]
    vmem = pl.BlockSpec(memory_space=pltpu.VMEM)
    any_space = pl.BlockSpec(memory_space=pl.ANY)
    smem = pl.BlockSpec(memory_space=pltpu.SMEM)
    n_q = n_dp // 2
    dma = pltpu.SemaphoreType.DMA
    probs, cot, image_grad, text_grad, loss = pl.pallas_call(
        functools.partial(forward_kernel, n_dp, n_mp, heads, embed),
        out_shape=(
            jax.ShapeDtypeStruct((heads, seq, seq), F32),
            jax.ShapeDtypeStruct((1, width), F32),
            jax.ShapeDtypeStruct((rows, embed), F32),
            jax.ShapeDtypeStruct((rows, embed), F32),
            jax.ShapeDtypeStruct((1, rows), F32),
        ),
        in_specs=[any_space] * 4 + [vmem] * 2 + [smem] * 5,
        out_specs=(any_space, vmem, vmem, vmem, vmem),
        scratch_shapes=[
            pltpu.VMEM(query_tokens.shape, BF16),
            pltpu.VMEM(query_tokens.shape, BF16),
            pltpu.VMEM(query_tokens.shape, BF16),
            pltpu.VMEM(head_weight.shape, BF16),
            pltpu.VMEM((n_dp, n_mp, 2 * rows, embed + 128), BF16),
            pltpu.VMEM((n_dp, n_mp * rows, embed), BF16),
            pltpu.VMEM((heads, seq, seq), F32),
            pltpu.VMEM((n_dp, 1, width), F32),
            pltpu.VMEM((n_mp, n_dp, cw), F32),
            pltpu.VMEM((n_dp, n_dp, cw), F32),
            pltpu.VMEM((n_dp, embed), F32),
            pltpu.VMEM((n_dp, 1, width), F32),
            pltpu.VMEM((n_dp, 1, width), F32),
            dma((4,)),
            dma((heads,)),
            dma((n_mp,)), dma((n_mp,)),
            dma((n_q,)), dma((n_q,)),
            dma((n_q,)), dma((n_q,)),
            dma((n_dp,)), dma((n_dp,)),
            dma((n_mp,)), dma((n_mp,)),
            dma((n_dp,)), dma((n_dp,)),
            dma((n_dp,)), dma((n_dp,)),
        ],
        compiler_params=pltpu.CompilerParams(
            collective_id=0, has_side_effects=True, vmem_limit_bytes=56 * 2**20),
        name="forward_pairs",
    )(
        query_tokens, key_tokens, value_tokens, head_weight, image_cache, text_embed,
        text_pair, image_group, text_group, logit_scale.reshape(1), logit_bias.reshape(1),
    )

    group = 2 if heads % 2 == 0 else 1
    token = pl.BlockSpec((1, seq, group * HEAD_DIM), lambda h: (0, 0, h))
    whole_rows = pl.BlockSpec((rows, embed), lambda h: (0, 0))
    whole_loss = pl.BlockSpec((1, rows), lambda h: (0, 0))
    query_grad, key_grad, value_grad, image_grad, text_grad, loss = pl.pallas_call(
        functools.partial(backward_kernel, group, seq),
        grid=(heads // group,),
        out_shape=(
            jax.ShapeDtypeStruct(query_tokens.shape, BF16),
            jax.ShapeDtypeStruct(query_tokens.shape, BF16),
            jax.ShapeDtypeStruct(query_tokens.shape, BF16),
            jax.ShapeDtypeStruct((rows, embed), F32),
            jax.ShapeDtypeStruct((rows, embed), F32),
            jax.ShapeDtypeStruct((1, rows), F32),
        ),
        in_specs=[
            token, token, token,
            pl.BlockSpec((group, seq, seq), lambda h: (h, 0, 0)),
            pl.BlockSpec((1, group * HEAD_DIM), lambda h: (0, h)),
            whole_rows, whole_rows, whole_loss,
        ],
        out_specs=(token, token, token, whole_rows, whole_rows, whole_loss),
        compiler_params=pltpu.CompilerParams(vmem_limit_bytes=56 * 2**20),
        name="attention_back",
    )(query_tokens, key_tokens, value_tokens, probs, cot, image_grad, text_grad, loss)
    return query_grad, key_grad, value_grad, image_grad, text_grad, loss.reshape(rows)


def solution(mesh):
    pair_rows = P(("dp", "mp"), None)
    pair = P(("dp", "mp"))
    tokens = P("dp", None, "mp")
    return jax.shard_map(
        functools.partial(on_device, mesh.shape["dp"], mesh.shape["mp"]),
        mesh=mesh,
        in_specs=(
            tokens, tokens, tokens, P("mp", "dp"), pair_rows, pair_rows, pair, pair, pair, P(), P(),
        ),
        out_specs=(tokens, tokens, tokens, pair_rows, pair_rows, pair),
        check_vma=False,
    )
```

time: 48 us -> 41.9 us (0.87)
  other arithmetic: 2.18 us -> 0 us
  Pallas kernels: 41.6 us -> 39.6 us
  local copies, waits for them, and re-layouts: 1.87 us -> 0 us
    select_n x3 -> x0, other arithmetic: 1.5 us -> none  [the longest x1 0.75 us: on_device(): second // LABEL_BASE]
    unnamed x8 -> x0, local copies, waits for them, and re-layouts: 1.24 us -> none
    pallas_call x1, Pallas kernels: 9.1 us -> 7.94 us  [on_device(): pl.pallas_call(functools.partial(backward_kernel, group, seq), grid=(head...]
    pallas_call x1, Pallas kernels: 32.5 us -> 31.7 us  [on_device(): pl.pallas_call(functools.partial(forward_kernel, n_dp, n_mp, heads, embed...]
    convert_element_type x1 -> x0, other arithmetic: 0.67 us -> none  [on_device(): labels = jnp.where(lane == 0, first // LABEL_BASE, jnp.where(lane == 1, f...]
    slice x1 -> x0, local copies, waits for them, and re-layouts: 0.63 us -> none  [on_device(): return (query_grad, key_grad, value_grad, image_grad, text_grad, loss[:, 0])]
where the time goes in v2:
time: 41.9 us; the launch traced here: 41.6 us
  Pallas kernels  39.6 us (95%)
  between operations  1.93 us (5%)
    pallas_call x1, Pallas kernels, on_device(): pl.pallas_call(functools.partial(forward_kernel, n_dp, n_mp, heads, embed...  31.7 us
    pallas_call x1, Pallas kernels, on_device(): pl.pallas_call(functools.partial(backward_kernel, group, seq), grid=(head...  7.94 us

profile of v2, /device:TPU:0, one launch (start us, length us, event | category | flops | bytes accessed | tf_op | source)
XLA Modules:
  0.0 41.6 jit_solution(3442691362423858849)
XLA Ops:
  1.9 31.7 %forward_pairs.1 = (f32[10,257,257]{2,1,0:T(8,128)}, f32[1,1280]{1,0:T(1,128)}, f32[8,1024]{1,0:T(8,128)}, f32[8,1024]{1,0:T(8,128)}, f32[1,8]{1,0:T(1,128)}) custom-call(bf16[1,257,1280]{2,1,0:T(8,128)(2,1)} %q_ref.1, bf16[1,257,1280]{2,1,0:T(8,128)(2,1)} %k_ref.1, bf16[1,257,1280]{2,1,0:T(8,128)(2,1)} %v_ref.1, bf16[1280,128]{1,0:T(8,128)(2,1)} %w_in.1, ...), custom_call_target="tpu_custom_call" | custom-call | tf_op jit(solution)/shard_map/forward_pairs/pallas_call | solution.py:368
  33.6 7.9 %attention_back.1 = (bf16[1,257,1280]{2,1,0:T(8,128)(2,1)}, bf16[1,257,1280]{2,1,0:T(8,128)(2,1)}, bf16[1,257,1280]{2,1,0:T(8,128)(2,1)}, f32[8,1024]{1,0:T(8,128)}, f32[8,1024]{1,0:T(8,128)}, /*index=5*/f32[1,8]{1,0:T(1,128)}) custom-call(bf16[1,257,1280]{2,1,0:T(8,128)(2,1)} %q_ref.1, bf16[1,257,1280]{2,1,0:T(8,128)(2,1)} %k_ref.1, ...), custom_call_target="tpu_custom_call" | custom-call | tf_op jit(solution)/shard_map/attention_back/pallas_call | solution.py:415

commit v3 on v2

--- a/solution.py
+++ b/solution.py
@@ -14,6 +14,7 @@
 F32 = jnp.float32
 BF16 = jnp.bfloat16
 LABEL_BASE = 64
+HEAD_ROWS = 16
 LOG2_E = 1.0 / math.log(2.0)
 DP_CHUNK = 8
 
@@ -26,8 +27,7 @@
         lax.fori_loop(1, count, lambda k, c: (body(k), c)[1], 0)
 
 
-def probs_t(queries, keys):
-    scores = lax.dot_general(keys, queries, (((1,), (1,)), ((), ())), preferred_element_type=F32)
+def softmax_t(scores):
     top = jnp.max(scores, axis=0, keepdims=True)
     grown = jnp.exp2((scores - top) * (INV_ROOT * LOG2_E))
     return grown * (1.0 / jnp.sum(grown, axis=0, keepdims=True))
@@ -36,6 +36,22 @@
 def column_mass(probs_low):
     ones = jnp.ones((probs_low.shape[1], HEAD_DIM), BF16)
     return jnp.dot(probs_low, ones, preferred_element_type=F32)
+
+
+def own_lanes(width):
+    shape = (HEAD_ROWS, width)
+    head = lax.broadcasted_iota(jnp.int32, shape, 0)
+    return lax.broadcasted_iota(jnp.int32, shape, 1) // HEAD_DIM == head
+
+
+def spread_heads(row):
+    wide = jnp.broadcast_to(row.astype(F32), (HEAD_ROWS, row.shape[1]))
+    return jnp.where(own_lanes(row.shape[1]), wide, 0.0).astype(BF16)
+
+
+def sum_heads(left, right):
+    full = lax.dot_general(left, right, (((0,), (0,)), ((), ())), preferred_element_type=F32)
+    return jnp.sum(jnp.where(own_lanes(right.shape[1]), full, 0.0), axis=0, keepdims=True)
 
 
 def pair_terms(scores, same, valid, temper, offset):
@@ -69,7 +85,7 @@
 def forward_kernel(
     n_dp, n_mp, heads, embed,
     q_in, k_in, v_in, w_in, img_ref, txt_ref, tpair_ref, igroup_ref, tgroup_ref, scale_ref, bias_ref,
-    p_out, cot_out, igrad_out, tgrad_out, loss_out,
+    p_out, last_out, cot_out, igrad_out, tgrad_out, loss_out,
     q_ref, k_ref, v_ref, w_ref, pairs, texts, probs, pooled, part, cols, fresh, sent, back,
     in_sem, p_sem, za_s, za_r, xb_s, xb_r, cc_s, cc_r, e2_s, e2_r, e3_s, e3_r, e5_s, e5_r, e4_s, e4_r,
 ):
@@ -81,6 +97,7 @@
     sibling = dp + 1 - 2 * core
     rows = img_ref.shape[0]
     seq = q_ref.shape[1]
+    main = seq - 1
     cw = w_ref.shape[1]
 
     def dp_at(k):
@@ -150,12 +167,17 @@
     for load in loads[:3]:
         load.wait()
 
+    last_p = softmax_t(nt_dot(k_ref[0], spread_heads(q_ref[0, main:, :])))
+    last_out[...] = last_p
+    last_mean = sum_heads(last_p.astype(BF16), v_ref[0])
+
     def head(h):
         at = slice(h * HEAD_DIM, (h + 1) * HEAD_DIM)
-        p = probs_t(q_ref[0, :, at], k_ref[0, :, at])
+        p = softmax_t(nt_dot(k_ref[0, :, at], q_ref[0, :main, at]))
         probs[h] = p
         mass = column_mass(p.astype(BF16))
-        mean = jnp.sum(mass * v_ref[0, :, at].astype(F32), axis=0, keepdims=True) * (1.0 / seq)
+        total = jnp.sum(mass * v_ref[0, :, at].astype(F32), axis=0, keepdims=True)
+        mean = (total + last_mean[:, at]) * (1.0 / seq)
         pooled[dp, :, at] = mean.astype(BF16).astype(F32)
 
     def keep(h):
@@ -323,32 +345,72 @@
 
 
 def backward_kernel(
-    group, seq,
-    q_ref, k_ref, v_ref, p_ref, cot_ref, igrad_ref, tgrad_ref, loss_ref,
-    qg_ref, kg_ref, vg_ref, igrad_out, tgrad_out, loss_out,
+    heads, group,
+    q_in, k_in, v_in, p_in, last_ref, cot_ref, igrad_ref, tgrad_ref, loss_ref,
+    qg_out, kg_out, vg_out, igrad_out, tgrad_out, loss_out,
+    q_ref, k_ref, v_ref, p_ref, qg_ref, kg_ref, vg_ref, in_sem, p_sem, out_sem,
 ):
-    @pl.when(pl.program_id(0) == 0)
-    def _():
-        igrad_out[...] = igrad_ref[...]
-        tgrad_out[...] = tgrad_ref[...]
-        loss_out[...] = loss_ref[...]
-
-    for h in range(group):
+    seq, width = q_ref.shape[1:]
+    main = seq - 1
+
+    def load_probs(h):
+        return pltpu.make_async_copy(p_in.at[h], p_ref.at[h], p_sem.at[h])
+
+    loads = [
+        pltpu.make_async_copy(src, dst, in_sem.at[i])
+        for i, (src, dst) in enumerate(((v_in, v_ref), (k_in, k_ref), (q_in, q_ref)))
+    ]
+    for load in loads:
+        load.start()
+    for h in range(heads):
+        load_probs(h).start()
+    igrad_out[...] = igrad_ref[...]
+    tgrad_out[...] = tgrad_ref[...]
+    loss_out[...] = loss_ref[...]
+    for load in loads:
+        load.wait()
+
+    def store(part, i):
+        ref, out = ((qg_ref, qg_out), (kg_ref, kg_out), (vg_ref, vg_out))[i]
+        at = pl.ds(part * group * HEAD_DIM, group * HEAD_DIM)
+        return pltpu.make_async_copy(ref.at[:, :, at], out.at[:, :, at], out_sem.at[i, part])
+
+    last_p = last_ref[...]
+    last_low = last_p.astype(BF16)
+    last_grad = nt_dot(v_ref[0], spread_heads(cot_ref[...]))
+    centre = jnp.sum(last_p * last_grad, axis=0, keepdims=True)
+    last_score = (last_p * (last_grad - centre)).astype(BF16)
+    last_query = spread_heads(q_ref[0, main:, :])
+    qg_ref[0, main:, :] = (sum_heads(last_score, k_ref[0]) * INV_ROOT).astype(BF16)
+    head_row = lax.broadcasted_iota(jnp.int32, (HEAD_ROWS, HEAD_DIM), 0)
+
+    for h in range(heads):
         at = slice(h * HEAD_DIM, (h + 1) * HEAD_DIM)
+        load_probs(h).wait()
         p = p_ref[h]
         cot = cot_ref[:, at]
         repeated = jnp.broadcast_to(cot, (HEAD_DIM, HEAD_DIM)).astype(BF16)
         prob_grad = nt_dot(v_ref[0, :, at], repeated)
-        prob_grad = jnp.concatenate([prob_grad] * pl.cdiv(seq, HEAD_DIM), axis=1)[:, :seq]
+        prob_grad = jnp.concatenate([prob_grad] * (main // HEAD_DIM), axis=1)
         centre = jnp.sum(p * prob_grad, axis=0, keepdims=True)
         score_grad = (p * (prob_grad - centre)).astype(BF16)
-        qg_ref[0, :, at] = (lax.dot_general(
+        qg_ref[0, :main, at] = (lax.dot_general(
             score_grad, k_ref[0, :, at], (((0,), (0,)), ((), ())), preferred_element_type=F32
         ) * INV_ROOT).astype(BF16)
-        kg_ref[0, :, at] = (jnp.dot(
-            score_grad, q_ref[0, :, at], preferred_element_type=F32
+        kg_ref[0, :, at] = ((
+            jnp.dot(score_grad, q_ref[0, :main, at], preferred_element_type=F32)
+            + jnp.dot(last_score, last_query[:, at], preferred_element_type=F32)
         ) * INV_ROOT).astype(BF16)
-        vg_ref[0, :, at] = (column_mass(p.astype(BF16)) * cot).astype(BF16)
+        pick = jnp.where(head_row == h, 1.0, 0.0).astype(BF16)
+        mass = column_mass(p.astype(BF16)) + jnp.dot(
+            last_low, pick, preferred_element_type=F32)
+        vg_ref[0, :, at] = (mass * cot).astype(BF16)
+        if (h + 1) % group == 0:
+            for i in range(3):
+                store(h // group, i).start()
+    for part in range(heads // group):
+        for i in range(3):
+            store(part, i).wait()
 
 
 def on_device(
@@ -365,17 +427,18 @@
     smem = pl.BlockSpec(memory_space=pltpu.SMEM)
     n_q = n_dp // 2
     dma = pltpu.SemaphoreType.DMA
-    probs, cot, image_grad, text_grad, loss = pl.pallas_call(
+    probs, last_probs, cot, image_grad, text_grad, loss = pl.pallas_call(
         functools.partial(forward_kernel, n_dp, n_mp, heads, embed),
         out_shape=(
-            jax.ShapeDtypeStruct((heads, seq, seq), F32),
+            jax.ShapeDtypeStruct((heads, seq, seq - 1), F32),
+            jax.ShapeDtypeStruct((seq, HEAD_ROWS), F32),
             jax.ShapeDtypeStruct((1, width), F32),
             jax.ShapeDtypeStruct((rows, embed), F32),
             jax.ShapeDtypeStruct((rows, embed), F32),
             jax.ShapeDtypeStruct((1, rows), F32),
         ),
         in_specs=[any_space] * 4 + [vmem] * 2 + [smem] * 5,
-        out_specs=(any_space, vmem, vmem, vmem, vmem),
+        out_specs=(any_space, vmem, vmem, vmem, vmem, vmem),
         scratch_shapes=[
             pltpu.VMEM(query_tokens.shape, BF16),
             pltpu.VMEM(query_tokens.shape, BF16),
@@ -383,7 +446,7 @@
             pltpu.VMEM(head_weight.shape, BF16),
             pltpu.VMEM((n_dp, n_mp, 2 * rows, embed + 128), BF16),
             pltpu.VMEM((n_dp, n_mp * rows, embed), BF16),
-            pltpu.VMEM((heads, seq, seq), F32),
+            pltpu.VMEM((heads, seq, seq - 1), F32),
             pltpu.VMEM((n_dp, 1, width), F32),
             pltpu.VMEM((n_mp, n_dp, cw), F32),
             pltpu.VMEM((n_dp, n_dp, cw), F32),
@@ -409,12 +472,8 @@
     )
 
     group = 2 if heads % 2 == 0 else 1
-    token = pl.BlockSpec((1, seq, group * HEAD_DIM), lambda h: (0, 0, h))
-    whole_rows = pl.BlockSpec((rows, embed), lambda h: (0, 0))
-    whole_loss = pl.BlockSpec((1, rows), lambda h: (0, 0))
     query_grad, key_grad, value_grad, image_grad, text_grad, loss = pl.pallas_call(
-        functools.partial(backward_kernel, group, seq),
-        grid=(heads // group,),
+        functools.partial(backward_kernel, heads, group),
         out_shape=(
             jax.ShapeDtypeStruct(query_tokens.shape, BF16),
             jax.ShapeDtypeStruct(query_tokens.shape, BF16),
@@ -423,16 +482,21 @@
             jax.ShapeDtypeStruct((rows, embed), F32),
             jax.ShapeDtypeStruct((1, rows), F32),
         ),
-        in_specs=[
-            token, token, token,
-            pl.BlockSpec((group, seq, seq), lambda h: (h, 0, 0)),
-            pl.BlockSpec((1, group * HEAD_DIM), lambda h: (0, h)),
-            whole_rows, whole_rows, whole_loss,
+        in_specs=[any_space] * 4 + [vmem] * 5,
+        out_specs=(any_space,) * 3 + (vmem,) * 3,
+        scratch_shapes=[
+            pltpu.VMEM(query_tokens.shape, BF16),
+            pltpu.VMEM(query_tokens.shape, BF16),
+            pltpu.VMEM(query_tokens.shape, BF16),
+            pltpu.VMEM((heads, seq, seq - 1), F32),
+            pltpu.VMEM(query_tokens.shape, BF16),
+            pltpu.VMEM(query_tokens.shape, BF16),
+            pltpu.VMEM(query_tokens.shape, BF16),
+            dma((3,)), dma((heads,)), dma((3, heads // group)),
         ],
-        out_specs=(token, token, token, whole_rows, whole_rows, whole_loss),
         compiler_params=pltpu.CompilerParams(vmem_limit_bytes=56 * 2**20),
         name="attention_back",
-    )(query_tokens, key_tokens, value_tokens, probs, cot, image_grad, text_grad, loss)
+    )(query_tokens, key_tokens, value_tokens, probs, last_probs, cot, image_grad, text_grad, loss)
     return query_grad, key_grad, value_grad, image_grad, text_grad, loss.reshape(rows)
 
 

time: 41.9 us -> 45.7 us (1.091)
  Pallas kernels: 39.6 us -> 43.5 us
    pallas_call x1, Pallas kernels: 7.94 us -> 11.8 us  [on_device(): pl.pallas_call(functools.partial(backward_kernel, heads, group), out_shap...]
where the time goes in v3:
time: 45.7 us; the launch traced here: 45.5 us
  Pallas kernels  43.5 us (95%)
  between operations  1.93 us (4%)
    pallas_call x1, Pallas kernels, on_device(): pl.pallas_call(functools.partial(forward_kernel, n_dp, n_mp, heads, embed...  31.7 us
    pallas_call x1, Pallas kernels, on_device(): pl.pallas_call(functools.partial(backward_kernel, heads, group), out_shap...  11.8 us

profile of v3, /device:TPU:0, one launch (start us, length us, event | category | flops | bytes accessed | tf_op | source)
XLA Modules:
  0.0 45.5 jit_solution(154708205523946832)
XLA Ops:
  1.9 31.7 %forward_pairs.1 = (f32[10,257,256]{2,1,0:T(8,128)}, f32[257,16]{1,0:T(8,128)}, f32[1,1280]{1,0:T(1,128)}, f32[8,1024]{1,0:T(8,128)}, f32[8,1024]{1,0:T(8,128)}, /*index=5*/f32[1,8]{1,0:T(1,128)}) custom-call(bf16[1,257,1280]{2,1,0:T(8,128)(2,1)} %q_in.3, bf16[1,257,1280]{2,1,0:T(8,128)(2,1)} %k_in.3, bf16[1,257,1280]{2,1,0:T(8,128)(2,1)} %v_in.3, ...), custom_call_target="tpu_custom_call" | custom-call | tf_op jit(solution)/shard_map/forward_pairs/pallas_call | solution.py:430
  33.7 11.8 %attention_back.1 = (bf16[1,257,1280]{2,1,0:T(8,128)(2,1)}, bf16[1,257,1280]{2,1,0:T(8,128)(2,1)}, bf16[1,257,1280]{2,1,0:T(8,128)(2,1)}, f32[8,1024]{1,0:T(8,128)}, f32[8,1024]{1,0:T(8,128)}, /*index=5*/f32[1,8]{1,0:T(1,128)}) custom-call(bf16[1,257,1280]{2,1,0:T(8,128)(2,1)} %q_in.3, bf16[1,257,1280]{2,1,0:T(8,128)(2,1)} %k_in.3, ...), custom_call_target="tpu_custom_call" | custom-call | tf_op jit(solution)/shard_map/attention_back/pallas_call | solution.py:475

commit v4 on v2

--- a/solution.py
+++ b/solution.py
@@ -14,6 +14,7 @@
 F32 = jnp.float32
 BF16 = jnp.bfloat16
 LABEL_BASE = 64
+HEAD_ROWS = 16
 LOG2_E = 1.0 / math.log(2.0)
 DP_CHUNK = 8
 
@@ -26,8 +27,7 @@
         lax.fori_loop(1, count, lambda k, c: (body(k), c)[1], 0)
 
 
-def probs_t(queries, keys):
-    scores = lax.dot_general(keys, queries, (((1,), (1,)), ((), ())), preferred_element_type=F32)
+def softmax_t(scores):
     top = jnp.max(scores, axis=0, keepdims=True)
     grown = jnp.exp2((scores - top) * (INV_ROOT * LOG2_E))
     return grown * (1.0 / jnp.sum(grown, axis=0, keepdims=True))
@@ -36,6 +36,23 @@
 def column_mass(probs_low):
     ones = jnp.ones((probs_low.shape[1], HEAD_DIM), BF16)
     return jnp.dot(probs_low, ones, preferred_element_type=F32)
+
+
+def own_lanes(width, start=0):
+    shape = (HEAD_ROWS, width)
+    head = lax.broadcasted_iota(jnp.int32, shape, 0)
+    return lax.broadcasted_iota(jnp.int32, shape, 1) // HEAD_DIM + start == head
+
+
+def spread_heads(row, start=0):
+    wide = jnp.broadcast_to(row.astype(F32), (HEAD_ROWS, row.shape[1]))
+    return jnp.where(own_lanes(row.shape[1], start), wide, 0.0).astype(BF16)
+
+
+def sum_heads(left, right, start=0):
+    full = lax.dot_general(left, right, (((0,), (0,)), ((), ())), preferred_element_type=F32)
+    own = own_lanes(right.shape[1], start)
+    return jnp.sum(jnp.where(own, full, 0.0), axis=0, keepdims=True)
 
 
 def pair_terms(scores, same, valid, temper, offset):
@@ -69,7 +86,7 @@
 def forward_kernel(
     n_dp, n_mp, heads, embed,
     q_in, k_in, v_in, w_in, img_ref, txt_ref, tpair_ref, igroup_ref, tgroup_ref, scale_ref, bias_ref,
-    p_out, cot_out, igrad_out, tgrad_out, loss_out,
+    p_out, last_out, cot_out, igrad_out, tgrad_out, loss_out,
     q_ref, k_ref, v_ref, w_ref, pairs, texts, probs, pooled, part, cols, fresh, sent, back,
     in_sem, p_sem, za_s, za_r, xb_s, xb_r, cc_s, cc_r, e2_s, e2_r, e3_s, e3_r, e5_s, e5_r, e4_s, e4_r,
 ):
@@ -81,6 +98,7 @@
     sibling = dp + 1 - 2 * core
     rows = img_ref.shape[0]
     seq = q_ref.shape[1]
+    main = seq - 1
     cw = w_ref.shape[1]
 
     def dp_at(k):
@@ -150,25 +168,37 @@
     for load in loads[:3]:
         load.wait()
 
+    last_p = softmax_t(nt_dot(k_ref[0], spread_heads(q_ref[0, main:, :])))
+    last_out[...] = last_p
+    last_mean = sum_heads(last_p.astype(BF16), v_ref[0])
+
     def head(h):
-        at = slice(h * HEAD_DIM, (h + 1) * HEAD_DIM)
-        p = probs_t(q_ref[0, :, at], k_ref[0, :, at])
+        at = pl.ds(pl.multiple_of(h * HEAD_DIM, HEAD_DIM), HEAD_DIM)
+        p = softmax_t(nt_dot(k_ref[0, :, at], q_ref[0, :main, at]))
         probs[h] = p
         mass = column_mass(p.astype(BF16))
-        mean = jnp.sum(mass * v_ref[0, :, at].astype(F32), axis=0, keepdims=True) * (1.0 / seq)
-        pooled[dp, :, at] = mean.astype(BF16).astype(F32)
+        pooled[dp, :, at] = jnp.sum(mass * v_ref[0, :, at].astype(F32), axis=0, keepdims=True)
 
     def keep(h):
         return pltpu.make_async_copy(probs.at[h], p_out.at[h], p_sem.at[h])
 
-    early = 2 * heads // 5
-    for h in range(early):
-        head(h)
-    each_peer(n_mp, lambda k: za(k, mp_from(k)).wait_recv())
-    each_peer(n_q, lambda k: xb(k, dp).start())
-    cc(0, dp).start()
-    for h in range(early, heads):
-        head(h)
+    group = 2 if heads % 2 == 0 else 1
+
+    def some_heads(i, carry):
+        for u in range(group):
+            head(i * group + u)
+
+        @pl.when(i == 1)
+        def _():
+            each_peer(n_mp, lambda k: za(k, mp_from(k)).wait_recv())
+            each_peer(n_q, lambda k: xb(k, dp).start())
+            cc(0, dp).start()
+
+        return carry
+
+    lax.fori_loop(0, heads // group, some_heads, 0)
+    mean = (pooled[dp] + last_mean) * (1.0 / seq)
+    pooled[dp] = mean.astype(BF16).astype(F32)
 
     def e2(k, slot):
         return remote(pooled.at[slot], pooled.at[slot], e2_s.at[k], e2_r.at[k], {"dp": dp_at(k)})
@@ -323,15 +353,27 @@
 
 
 def backward_kernel(
-    group, seq,
-    q_ref, k_ref, v_ref, p_ref, cot_ref, igrad_ref, tgrad_ref, loss_ref,
+    group,
+    q_ref, k_ref, v_ref, p_ref, last_ref, cot_ref, igrad_ref, tgrad_ref, loss_ref,
     qg_ref, kg_ref, vg_ref, igrad_out, tgrad_out, loss_out,
 ):
+    main = q_ref.shape[1] - 1
+    start = pl.program_id(0) * group
+
     @pl.when(pl.program_id(0) == 0)
     def _():
         igrad_out[...] = igrad_ref[...]
         tgrad_out[...] = tgrad_ref[...]
         loss_out[...] = loss_ref[...]
+
+    last_p = last_ref[...]
+    last_low = last_p.astype(BF16)
+    last_grad = nt_dot(v_ref[0], spread_heads(cot_ref[...], start))
+    centre = jnp.sum(last_p * last_grad, axis=0, keepdims=True)
+    last_score = (last_p * (last_grad - centre)).astype(BF16)
+    last_query = spread_heads(q_ref[0, main:, :], start)
+    qg_ref[0, main:, :] = (sum_heads(last_score, k_ref[0], start) * INV_ROOT).astype(BF16)
+    head_row = lax.broadcasted_iota(jnp.int32, (HEAD_ROWS, HEAD_DIM), 0)
 
     for h in range(group):
         at = slice(h * HEAD_DIM, (h + 1) * HEAD_DIM)
@@ -339,16 +381,20 @@
         cot = cot_ref[:, at]
         repeated = jnp.broadcast_to(cot, (HEAD_DIM, HEAD_DIM)).astype(BF16)
         prob_grad = nt_dot(v_ref[0, :, at], repeated)
-        prob_grad = jnp.concatenate([prob_grad] * pl.cdiv(seq, HEAD_DIM), axis=1)[:, :seq]
+        prob_grad = jnp.concatenate([prob_grad] * (main // HEAD_DIM), axis=1)
         centre = jnp.sum(p * prob_grad, axis=0, keepdims=True)
         score_grad = (p * (prob_grad - centre)).astype(BF16)
-        qg_ref[0, :, at] = (lax.dot_general(
+        qg_ref[0, :main, at] = (lax.dot_general(
             score_grad, k_ref[0, :, at], (((0,), (0,)), ((), ())), preferred_element_type=F32
         ) * INV_ROOT).astype(BF16)
-        kg_ref[0, :, at] = (jnp.dot(
-            score_grad, q_ref[0, :, at], preferred_element_type=F32
+        kg_ref[0, :, at] = ((
+            jnp.dot(score_grad, q_ref[0, :main, at], preferred_element_type=F32)
+            + jnp.dot(last_score, last_query[:, at], preferred_element_type=F32)
         ) * INV_ROOT).astype(BF16)
-        vg_ref[0, :, at] = (column_mass(p.astype(BF16)) * cot).astype(BF16)
+        pick = jnp.where(head_row == start + h, 1.0, 0.0).astype(BF16)
+        mass = column_mass(p.astype(BF16)) + jnp.dot(
+            last_low, pick, preferred_element_type=F32)
+        vg_ref[0, :, at] = (mass * cot).astype(BF16)
 
 
 def on_device(
@@ -365,17 +411,18 @@
     smem = pl.BlockSpec(memory_space=pltpu.SMEM)
     n_q = n_dp // 2
     dma = pltpu.SemaphoreType.DMA
-    probs, cot, image_grad, text_grad, loss = pl.pallas_call(
+    probs, last_probs, cot, image_grad, text_grad, loss = pl.pallas_call(
         functools.partial(forward_kernel, n_dp, n_mp, heads, embed),
         out_shape=(
-            jax.ShapeDtypeStruct((heads, seq, seq), F32),
+            jax.ShapeDtypeStruct((heads, seq, seq - 1), F32),
+            jax.ShapeDtypeStruct((seq, HEAD_ROWS), F32),
             jax.ShapeDtypeStruct((1, width), F32),
             jax.ShapeDtypeStruct((rows, embed), F32),
             jax.ShapeDtypeStruct((rows, embed), F32),
             jax.ShapeDtypeStruct((1, rows), F32),
         ),
         in_specs=[any_space] * 4 + [vmem] * 2 + [smem] * 5,
-        out_specs=(any_space, vmem, vmem, vmem, vmem),
+        out_specs=(any_space, vmem, vmem, vmem, vmem, vmem),
         scratch_shapes=[
             pltpu.VMEM(query_tokens.shape, BF16),
             pltpu.VMEM(query_tokens.shape, BF16),
@@ -383,7 +430,7 @@
             pltpu.VMEM(head_weight.shape, BF16),
             pltpu.VMEM((n_dp, n_mp, 2 * rows, embed + 128), BF16),
             pltpu.VMEM((n_dp, n_mp * rows, embed), BF16),
-            pltpu.VMEM((heads, seq, seq), F32),
+            pltpu.VMEM((heads, seq, seq - 1), F32),
             pltpu.VMEM((n_dp, 1, width), F32),
             pltpu.VMEM((n_mp, n_dp, cw), F32),
             pltpu.VMEM((n_dp, n_dp, cw), F32),
@@ -413,7 +460,7 @@
     whole_rows = pl.BlockSpec((rows, embed), lambda h: (0, 0))
     whole_loss = pl.BlockSpec((1, rows), lambda h: (0, 0))
     query_grad, key_grad, value_grad, image_grad, text_grad, loss = pl.pallas_call(
-        functools.partial(backward_kernel, group, seq),
+        functools.partial(backward_kernel, group),
         grid=(heads // group,),
         out_shape=(
             jax.ShapeDtypeStruct(query_tokens.shape, BF16),
@@ -425,14 +472,15 @@
         ),
         in_specs=[
             token, token, token,
-            pl.BlockSpec((group, seq, seq), lambda h: (h, 0, 0)),
+            pl.BlockSpec((group, seq, seq - 1), lambda h: (h, 0, 0)),
+            pl.BlockSpec((seq, HEAD_ROWS), lambda h: (0, 0)),
             pl.BlockSpec((1, group * HEAD_DIM), lambda h: (0, h)),
             whole_rows, whole_rows, whole_loss,
         ],
         out_specs=(token, token, token, whole_rows, whole_rows, whole_loss),
         compiler_params=pltpu.CompilerParams(vmem_limit_bytes=56 * 2**20),
         name="attention_back",
-    )(query_tokens, key_tokens, value_tokens, probs, cot, image_grad, text_grad, loss)
+    )(query_tokens, key_tokens, value_tokens, probs, last_probs, cot, image_grad, text_grad, loss)
     return query_grad, key_grad, value_grad, image_grad, text_grad, loss.reshape(rows)
 
 

time: 41.9 us -> 42.3 us (level)
  Pallas kernels: 39.6 us -> 40.1 us
where the time goes in v4:
time: 42.3 us; the launch traced here: 42 us
  Pallas kernels  40.1 us (95%)
  between operations  1.93 us (5%)
    pallas_call x1, Pallas kernels, on_device(): pl.pallas_call(functools.partial(forward_kernel, n_dp, n_mp, heads, embed...  31.7 us
    pallas_call x1, Pallas kernels, on_device(): pl.pallas_call(functools.partial(backward_kernel, group), grid=(heads //...  8.35 us

profile of v4, /device:TPU:0, one launch (start us, length us, event | category | flops | bytes accessed | tf_op | source)
XLA Modules:
  0.0 42.0 jit_solution(8558461012782708001)
XLA Ops:
  1.9 31.7 %forward_pairs.1 = (f32[10,257,256]{2,1,0:T(8,128)}, f32[257,16]{1,0:T(8,128)}, f32[1,1280]{1,0:T(1,128)}, f32[8,1024]{1,0:T(8,128)}, f32[8,1024]{1,0:T(8,128)}, /*index=5*/f32[1,8]{1,0:T(1,128)}) custom-call(bf16[1,257,1280]{2,1,0:T(8,128)(2,1)} %q_ref.1, bf16[1,257,1280]{2,1,0:T(8,128)(2,1)} %k_ref.1, bf16[1,257,1280]{2,1,0:T(8,128)(2,1)} %v_ref.1, ...), custom_call_target="tpu_custom_call" | custom-call | tf_op jit(solution)/shard_map/forward_pairs/pallas_call | solution.py:414
  33.7 8.4 %attention_back.1 = (bf16[1,257,1280]{2,1,0:T(8,128)(2,1)}, bf16[1,257,1280]{2,1,0:T(8,128)(2,1)}, bf16[1,257,1280]{2,1,0:T(8,128)(2,1)}, f32[8,1024]{1,0:T(8,128)}, f32[8,1024]{1,0:T(8,128)}, /*index=5*/f32[1,8]{1,0:T(1,128)}) custom-call(bf16[1,257,1280]{2,1,0:T(8,128)(2,1)} %q_ref.1, bf16[1,257,1280]{2,1,0:T(8,128)(2,1)} %k_ref.1, ...), custom_call_target="tpu_custom_call" | custom-call | tf_op jit(solution)/shard_map/attention_back/pallas_call | solution.py:462

commit v5 on v4

--- a/solution.py
+++ b/solution.py
@@ -16,7 +16,6 @@
 LABEL_BASE = 64
 HEAD_ROWS = 16
 LOG2_E = 1.0 / math.log(2.0)
-DP_CHUNK = 8
 
 
 def each_peer(count, body):
@@ -87,8 +86,8 @@
     n_dp, n_mp, heads, embed,
     q_in, k_in, v_in, w_in, img_ref, txt_ref, tpair_ref, igroup_ref, tgroup_ref, scale_ref, bias_ref,
     p_out, last_out, cot_out, igrad_out, tgrad_out, loss_out,
-    q_ref, k_ref, v_ref, w_ref, pairs, texts, probs, pooled, part, cols, fresh, sent, back,
-    in_sem, p_sem, za_s, za_r, xb_s, xb_r, cc_s, cc_r, e2_s, e2_r, e3_s, e3_r, e5_s, e5_r, e4_s, e4_r,
+    q_ref, k_ref, v_ref, w_ref, tslots, islots, table, probs, pooled, part, cols, fresh, sent, back,
+    in_sem, p_sem, za_s, za_r, xb_s, xb_r, cc_s, cc_r, iza_s, iza_r, ixb_s, ixb_r, icc_s, icc_r, e2_s, e2_r, e3_s, e3_r, e5_s, e5_r, e4_s, e4_r,
 ):
     dp = lax.axis_index("dp")
     mp = lax.axis_index("mp")
@@ -134,19 +133,28 @@
 
     raw = jnp.concatenate([img_ref[...].astype(F32), txt_ref[...].astype(F32)], axis=0)
     norm = lax.rsqrt(jnp.sum(raw * raw, axis=1, keepdims=True) + 1e-06)
-    pairs[dp, mp, :, :embed] = (raw * norm).astype(BF16)
+    unit = raw * norm
+    half = embed // 2
     spot = lax.broadcasted_iota(jnp.int32, (2 * rows, 128), 0)
     lane = lax.broadcasted_iota(jnp.int32, (2 * rows, 128), 1)
     first = (dp * n_mp + mp) * rows + spot
     second = jnp.zeros_like(spot)
+    third = jnp.zeros_like(spot)
     for r in range(rows):
         first = jnp.where(spot == rows + r, tpair_ref[r], first)
         second = jnp.where(spot == r, igroup_ref[r], second)
         second = jnp.where(spot == rows + r, tgroup_ref[r], second)
-    label = jnp.where(lane < 2, first, second)
+        third = jnp.where(spot == rows + r, igroup_ref[r], third)
+    label = jnp.where(lane < 2, first, jnp.where(lane < 4, second, third))
     own_tags = jnp.where(lax.rem(lane, 2) == 0, label // LABEL_BASE, lax.rem(label, LABEL_BASE))
     own_tags = own_tags.astype(F32)
-    pairs[dp, mp, :, embed:] = own_tags.astype(BF16)
+
+    for slots, lo in ((islots, 0), (tslots, rows)):
+        mine = unit[lo:lo + rows]
+        slots[dp, mp, :, :half] = jnp.concatenate(
+            [mine[:, :half], mine[:, half:]], axis=0).astype(BF16)
+        tags = own_tags[lo:lo + rows]
+        slots[dp, mp, :, half:] = jnp.concatenate([tags, tags], axis=0).astype(BF16)
     pl.semaphore_wait(barrier, n_mp - 1 + n_dp - 1)
 
     def remote(src, dst, s_sem, r_sem, target):
@@ -154,16 +162,50 @@
             src_ref=src, dst_ref=dst, send_sem=s_sem, recv_sem=r_sem,
             device_id=target, device_id_type=pl.DeviceIdType.MESH)
 
-    def za(k, slot):
-        return remote(pairs.at[dp, slot], pairs.at[dp, slot], za_s.at[k], za_r.at[k], {"mp": mp_at(k)})
-
-    def xb(k, block):
-        return remote(pairs.at[block], pairs.at[block], xb_s.at[k], xb_r.at[k], {"dp": chip_at(k)})
-
-    def cc(k, block):
-        return remote(pairs.at[block], pairs.at[block], cc_s.at[k], cc_r.at[k], {"dp": sibling})
-
-    each_peer(n_mp, lambda k: za(k, mp).start())
+    def spread(slots, za_s, za_r, xb_s, xb_r, cc_s, cc_r):
+        def za(k, slot):
+            at = slots.at[dp, slot]
+            return remote(at, at, za_s.at[k], za_r.at[k], {"mp": mp_at(k)})
+
+        def xb(k, block):
+            return remote(slots.at[block], slots.at[block], xb_s.at[k], xb_r.at[k], {"dp": chip_at(k)})
+
+        def cc(k, block):
+            return remote(slots.at[block], slots.at[block], cc_s.at[k], cc_r.at[k], {"dp": sibling})
+
+        def along():
+            each_peer(n_mp, lambda k: za(k, mp_from(k)).wait_recv())
+            each_peer(n_q, lambda k: xb(k, dp).start())
+            cc(0, dp).start()
+
+        def relay(k):
+            xb(k, chip_from(k)).wait_recv()
+            cc(k, chip_from(k)).start()
+
+        def settle(k):
+            block = 2 * lax.rem(q_me + n_q - k, n_q) + 1 - core
+            cc(k, block).wait_recv()
+
+        def settle_all():
+            settle(0)
+            each_peer(n_q, settle)
+
+        def drain():
+            each_peer(n_mp, lambda k: za(k, mp).wait_send())
+            each_peer(n_q, lambda k: xb(k, dp).wait_send())
+            cc(0, dp).wait_send()
+            each_peer(n_q, lambda k: cc(k, chip_from(k)).wait_send())
+
+        begin = lambda: each_peer(n_mp, lambda k: za(k, mp).start())
+        return begin, along, lambda: each_peer(n_q, relay), settle_all, drain
+
+    t_begin, t_along, t_relay, t_settle, t_drain = spread(
+        tslots, za_s, za_r, xb_s, xb_r, cc_s, cc_r)
+    i_begin, i_along, i_relay, i_settle, i_drain = spread(
+        islots, iza_s, iza_r, ixb_s, ixb_r, icc_s, icc_r)
+
+    t_begin()
+    i_begin()
 
     for load in loads[:3]:
         load.wait()
@@ -190,9 +232,7 @@
 
         @pl.when(i == 1)
         def _():
-            each_peer(n_mp, lambda k: za(k, mp_from(k)).wait_recv())
-            each_peer(n_q, lambda k: xb(k, dp).start())
-            cc(0, dp).start()
+            t_along()
 
         return carry
 
@@ -204,9 +244,10 @@
         return remote(pooled.at[slot], pooled.at[slot], e2_s.at[k], e2_r.at[k], {"dp": dp_at(k)})
 
     each_peer(n_dp, lambda k: e2(k, dp).start())
-
+    i_along()
     for h in range(heads):
         keep(h).start()
+    t_relay()
     loads[3].wait()
     each_peer(n_dp, lambda k: e2(k, dp_from(k)).wait_recv())
     every = pooled[...].reshape(n_dp, heads * HEAD_DIM).astype(BF16)
@@ -217,11 +258,6 @@
 
     each_peer(n_mp, lambda k: e3(k, mp).start())
 
-    def relay(k):
-        xb(k, chip_from(k)).wait_recv()
-        cc(k, chip_from(k)).start()
-
-    each_peer(n_q, relay)
     each_peer(n_mp, lambda k: e3(k, mp_from(k)).wait_recv())
     cols[dp] = jnp.sum(part[...], axis=0)
 
@@ -230,60 +266,46 @@
 
     each_peer(n_dp, lambda k: e5(k, dp).start())
 
-    def settle(k):
-        block = 2 * lax.rem(q_me + n_q - k, n_q) + 1 - core
-        cc(k, block).wait_recv()
-
-    settle(0)
-    each_peer(n_q, settle)
-
-    unit = raw * norm
+    t_settle()
+
+    def gather(slots, whole, b):
+        wide = slots[b].astype(F32)
+        left = wide[:, :rows, :half].reshape(n_mp * rows, half)
+        right = wide[:, rows:, :half].reshape(n_mp * rows, half)
+        whole[b] = jnp.concatenate([left, right], axis=1).astype(BF16)
+
+    def gather_all(slots, whole):
+        gather(slots, whole, 0)
+        each_peer(n_dp, lambda b: gather(slots, whole, b))
+
+    def tags_of(slots):
+        return slots[:, :, :, half:].astype(F32)[:, :, :rows].reshape(n_dp * n_mp * rows, 128)
+
+    def all_rows():
+        return table[...].reshape(n_dp * n_mp * rows, embed)
+
+    gather_all(tslots, table)
     low = unit.astype(BF16)
+    unit_image, unit_text = unit[:rows], unit[rows:]
     temper = jnp.exp(jnp.full((1, 1), scale_ref[0], F32))
     offset = bias_ref[0]
     own_a, own_b = row_labels(own_tags)
-    own_text = lax.broadcasted_iota(jnp.int32, (2 * rows, 1), 0) >= rows
-    step = min(DP_CHUNK, n_dp)
-    wide = step * n_mp * 2 * rows
-
-    def chunk(at):
-        block = pairs[pl.ds(at * step, step), :, :, :embed].reshape(wide, embed)
-        col_a, col_b = lane_labels(
-            pairs[pl.ds(at * step, step), :, :, embed:].reshape(wide, 128).astype(F32))
-        spot = lax.broadcasted_iota(jnp.int32, (1, wide), 1)
-        col_text = lax.rem(spot, 2 * rows) >= rows
-        valid = (own_text != col_text) & (lax.rem(spot, n_mp * 2 * rows) != 0)
-        same = (own_a == col_a) | (own_b == col_b)
-        coeffs, losses = pair_terms(nt_dot(low, block), same, valid, temper, offset)
-        return jnp.dot(coeffs, block, preferred_element_type=F32), losses
-
-    if n_dp == step:
-        direction, losses = chunk(0)
-    else:
-        def more(at, carry):
-            new = chunk(at)
-            return carry[0] + new[0], carry[1] + new[1]
-        direction, losses = lax.fori_loop(
-            0, n_dp // step, more,
-            (jnp.zeros((2 * rows, embed), F32), jnp.zeros((2 * rows, 1), F32)))
-
-    def copy_texts(b):
-        texts[b] = pairs[b, :, :, :embed].astype(F32)[:, rows:].reshape(
-            n_mp * rows, embed).astype(BF16)
-
-    copy_texts(0)
-    each_peer(n_dp, copy_texts)
-    text_a, text_b = lane_labels(
-        pairs[:, :, :, embed:].astype(F32)[:, :, rows:].reshape(n_dp * n_mp * rows, 128))
-    tags = pairs[:, 0, :, embed:].astype(F32)
+    text_a, text_b = lane_labels(tags_of(tslots))
+    coeffs, losses = pair_terms(
+        nt_dot(low[:rows], all_rows()),
+        (own_a[:rows] == text_a) | (own_b[:rows] == text_b), None, temper, offset)
+    image_dir = jnp.dot(coeffs, all_rows(), preferred_element_type=F32)
+    image_grad = (
+        image_dir - unit_image * jnp.sum(unit_image * image_dir, axis=1, keepdims=True)
+    ) * norm[:rows]
+    i_relay()
+
+    tags = tslots[:, 0, :, half:].astype(F32)
     lead = lax.broadcasted_iota(jnp.int32, tags.shape, 1) == 0
     fresh_tags = jnp.sum(jnp.where(lead, tags, 0.0), axis=1)
-    fresh_a, fresh_b = row_labels(fresh_tags)
-    fresh_lane_a, fresh_lane_b = lane_labels(fresh_tags)
+    fresh_a = (lax.broadcasted_iota(jnp.int32, (n_dp, 1), 0) * (n_mp * rows)).astype(F32)
+    fresh_b = fresh_tags[:, 4:5] * LABEL_BASE + fresh_tags[:, 5:6]
     fresh_same = (fresh_a == text_a) | (fresh_b == text_b)
-    back_same = (own_a[rows:] == fresh_lane_a) | (own_b[rows:] == fresh_lane_b)
-    all_texts = texts[...].reshape(n_dp * n_mp * rows, embed)
-
     each_peer(n_dp, lambda k: e5(k, dp_from(k)).wait_recv())
     for c in range(n_dp):
         fresh[:, c * cw:(c + 1) * cw] = cols[c]
@@ -292,8 +314,8 @@
     unit_fresh = raw_fresh * fresh_norm
     low_fresh = unit_fresh.astype(BF16)
     coeffs, fresh_loss = pair_terms(
-        nt_dot(low_fresh, all_texts), fresh_same, None, temper, offset)
-    fresh_dir = jnp.dot(coeffs, all_texts, preferred_element_type=F32)
+        nt_dot(low_fresh, all_rows()), fresh_same, None, temper, offset)
+    fresh_dir = jnp.dot(coeffs, all_rows(), preferred_element_type=F32)
     fresh_grad = (
         fresh_dir - unit_fresh * jnp.sum(unit_fresh * fresh_dir, axis=1, keepdims=True)
     ) * fresh_norm
@@ -317,18 +339,26 @@
 
     each_peer(n_dp, lambda k: e4(k, dp_at(k), dp).start())
 
+    i_settle()
+    gather_all(islots, table)
+    image_a, image_b = lane_labels(tags_of(islots))
+    fresh_lane_a = (lax.broadcasted_iota(jnp.int32, (1, n_dp), 1) * (n_mp * rows)).astype(F32)
+    fresh_turned = fresh_tags.T
+    fresh_lane_b = fresh_turned[4:5] * LABEL_BASE + fresh_turned[5:6]
+    stale = lax.rem(
+        lax.broadcasted_iota(jnp.int32, (1, n_dp * n_mp * rows), 1), n_mp * rows) == 0
     coeffs, unused = pair_terms(
-        nt_dot(low[rows:], low_fresh), back_same, None, temper, offset)
-    added = jnp.dot(coeffs, low_fresh, preferred_element_type=F32)
-    text_dir = direction[rows:] + added
-    unit_text = unit[rows:]
+        nt_dot(low[rows:], all_rows()),
+        (own_a[rows:] == image_a) | (own_b[rows:] == image_b),
+        jnp.logical_not(stale), temper, offset)
+    text_dir = jnp.dot(coeffs, all_rows(), preferred_element_type=F32)
+    coeffs, unused = pair_terms(
+        nt_dot(low[rows:], low_fresh),
+        (own_a[rows:] == fresh_lane_a) | (own_b[rows:] == fresh_lane_b), None, temper, offset)
+    text_dir = text_dir + jnp.dot(coeffs, low_fresh, preferred_element_type=F32)
     tgrad_out[...] = (
         text_dir - unit_text * jnp.sum(unit_text * text_dir, axis=1, keepdims=True)
     ) * norm[rows:]
-    unit_image, image_dir = unit[:rows], direction[:rows]
-    image_grad = (
-        image_dir - unit_image * jnp.sum(unit_image * image_dir, axis=1, keepdims=True)
-    ) * norm[:rows]
     is_fresh = (lax.broadcasted_iota(jnp.int32, (rows, 1), 0) == 0) & (mp == 0)
     fresh[...] = fresh_grad
     igrad_out[...] = jnp.where(is_fresh, fresh[pl.ds(dp, 1), :], image_grad)
@@ -339,10 +369,8 @@
 
     for h in range(heads):
         keep(h).wait()
-    each_peer(n_mp, lambda k: za(k, mp).wait_send())
-    each_peer(n_q, lambda k: xb(k, dp).wait_send())
-    cc(0, dp).wait_send()
-    each_peer(n_q, lambda k: cc(k, chip_from(k)).wait_send())
+    t_drain()
+    i_drain()
     each_peer(n_dp, lambda k: e2(k, dp).wait_send())
     each_peer(n_mp, lambda k: e3(k, mp).wait_send())
     each_peer(n_dp, lambda k: e5(k, dp).wait_send())
@@ -428,7 +456,8 @@
             pltpu.VMEM(query_tokens.shape, BF16),
             pltpu.VMEM(query_tokens.shape, BF16),
             pltpu.VMEM(head_weight.shape, BF16),
-            pltpu.VMEM((n_dp, n_mp, 2 * rows, embed + 128), BF16),
+            pltpu.VMEM((n_dp, n_mp, 2 * rows, embed // 2 + 128), BF16),
+            pltpu.VMEM((n_dp, n_mp, 2 * rows, embed // 2 + 128), BF16),
             pltpu.VMEM((n_dp, n_mp * rows, embed), BF16),
             pltpu.VMEM((heads, seq, seq - 1), F32),
             pltpu.VMEM((n_dp, 1, width), F32),
@@ -439,6 +468,9 @@
             pltpu.VMEM((n_dp, 1, width), F32),
             dma((4,)),
             dma((heads,)),
+            dma((n_mp,)), dma((n_mp,)),
+            dma((n_q,)), dma((n_q,)),
+            dma((n_q,)), dma((n_q,)),
             dma((n_mp,)), dma((n_mp,)),
             dma((n_q,)), dma((n_q,)),
             dma((n_q,)), dma((n_q,)),

time: 42.3 us -> 41 us (0.969)
  Pallas kernels: 40.1 us -> 38.7 us
    pallas_call x1, Pallas kernels: 31.7 us -> 30.4 us  [on_device(): pl.pallas_call(functools.partial(forward_kernel, n_dp, n_mp, heads, embed...]
where the time goes in v5:
time: 41 us; the launch traced here: 40.7 us
  Pallas kernels  38.7 us (94%)
  between operations  1.93 us (5%)
    pallas_call x1, Pallas kernels, on_device(): pl.pallas_call(functools.partial(forward_kernel, n_dp, n_mp, heads, embed...  30.4 us
    pallas_call x1, Pallas kernels, on_device(): pl.pallas_call(functools.partial(backward_kernel, group), grid=(heads //...  8.35 us

profile of v5, /device:TPU:0, one launch (start us, length us, event | category | flops | bytes accessed | tf_op | source)
XLA Modules:
  0.0 40.7 jit_solution(14105671806974950708)
XLA Ops:
  1.9 30.4 %forward_pairs.1 = (f32[10,257,256]{2,1,0:T(8,128)}, f32[257,16]{1,0:T(8,128)}, f32[1,1280]{1,0:T(1,128)}, f32[8,1024]{1,0:T(8,128)}, f32[8,1024]{1,0:T(8,128)}, /*index=5*/f32[1,8]{1,0:T(1,128)}) custom-call(bf16[1,257,1280]{2,1,0:T(8,128)(2,1)} %q_ref.1, bf16[1,257,1280]{2,1,0:T(8,128)(2,1)} %k_ref.1, bf16[1,257,1280]{2,1,0:T(8,128)(2,1)} %v_ref.1, ...), custom_call_target="tpu_custom_call" | custom-call | tf_op jit(solution)/shard_map/forward_pairs/pallas_call | solution.py:442
  32.3 8.4 %attention_back.1 = (bf16[1,257,1280]{2,1,0:T(8,128)(2,1)}, bf16[1,257,1280]{2,1,0:T(8,128)(2,1)}, bf16[1,257,1280]{2,1,0:T(8,128)(2,1)}, f32[8,1024]{1,0:T(8,128)}, f32[8,1024]{1,0:T(8,128)}, /*index=5*/f32[1,8]{1,0:T(1,128)}) custom-call(bf16[1,257,1280]{2,1,0:T(8,128)(2,1)} %q_ref.1, bf16[1,257,1280]{2,1,0:T(8,128)(2,1)} %k_ref.1, ...), custom_call_target="tpu_custom_call" | custom-call | tf_op jit(solution)/shard_map/attention_back/pallas_call | solution.py:494

commit v6 on v5

--- a/solution.py
+++ b/solution.py
@@ -33,8 +33,7 @@
 
 
 def column_mass(probs_low):
-    ones = jnp.ones((probs_low.shape[1], HEAD_DIM), BF16)
-    return jnp.dot(probs_low, ones, preferred_element_type=F32)
+    return jnp.sum(probs_low.astype(F32), axis=1, keepdims=True)
 
 
 def own_lanes(width, start=0):
@@ -399,17 +398,19 @@
     last_grad = nt_dot(v_ref[0], spread_heads(cot_ref[...], start))
     centre = jnp.sum(last_p * last_grad, axis=0, keepdims=True)
     last_score = (last_p * (last_grad - centre)).astype(BF16)
-    last_query = spread_heads(q_ref[0, main:, :], start)
     qg_ref[0, main:, :] = (sum_heads(last_score, k_ref[0], start) * INV_ROOT).astype(BF16)
-    head_row = lax.broadcasted_iota(jnp.int32, (HEAD_ROWS, HEAD_DIM), 0)
+    head_lane = lax.broadcasted_iota(jnp.int32, last_p.shape, 1)
 
     for h in range(group):
         at = slice(h * HEAD_DIM, (h + 1) * HEAD_DIM)
         p = p_ref[h]
         cot = cot_ref[:, at]
-        repeated = jnp.broadcast_to(cot, (HEAD_DIM, HEAD_DIM)).astype(BF16)
-        prob_grad = nt_dot(v_ref[0, :, at], repeated)
-        prob_grad = jnp.concatenate([prob_grad] * (main // HEAD_DIM), axis=1)
+        mine = head_lane == start + h
+
+        def column(table):
+            return jnp.sum(jnp.where(mine, table.astype(F32), 0.0), axis=1, keepdims=True)
+
+        prob_grad = column(last_grad)
         centre = jnp.sum(p * prob_grad, axis=0, keepdims=True)
         score_grad = (p * (prob_grad - centre)).astype(BF16)
         qg_ref[0, :main, at] = (lax.dot_general(
@@ -417,11 +418,9 @@
         ) * INV_ROOT).astype(BF16)
         kg_ref[0, :, at] = ((
             jnp.dot(score_grad, q_ref[0, :main, at], preferred_element_type=F32)
-            + jnp.dot(last_score, last_query[:, at], preferred_element_type=F32)
+            + column(last_score) * q_ref[0, main:, at].astype(F32)
         ) * INV_ROOT).astype(BF16)
-        pick = jnp.where(head_row == start + h, 1.0, 0.0).astype(BF16)
-        mass = column_mass(p.astype(BF16)) + jnp.dot(
-            last_low, pick, preferred_element_type=F32)
+        mass = column_mass(p.astype(BF16)) + column(last_low)
         vg_ref[0, :, at] = (mass * cot).astype(BF16)
 
 

time: 41 us -> 39.5 us (0.963)
  Pallas kernels: 38.7 us -> 37.2 us
    pallas_call x1, Pallas kernels: 8.35 us -> 6.92 us  [on_device(): pl.pallas_call(functools.partial(backward_kernel, group), grid=(heads //...]
where the time goes in v6:
time: 39.5 us; the launch traced here: 39.1 us
  Pallas kernels  37.2 us (94%)
  between operations  1.93 us (5%)
    pallas_call x1, Pallas kernels, on_device(): pl.pallas_call(functools.partial(forward_kernel, n_dp, n_mp, heads, embed...  30.3 us
    pallas_call x1, Pallas kernels, on_device(): pl.pallas_call(functools.partial(backward_kernel, group), grid=(heads //...  6.92 us

profile of v6, /device:TPU:0, one launch (start us, length us, event | category | flops | bytes accessed | tf_op | source)
XLA Modules:
  0.0 39.1 jit_solution(7471763080889636139)
XLA Ops:
  1.9 30.3 %forward_pairs.1 = (f32[10,257,256]{2,1,0:T(8,128)}, f32[257,16]{1,0:T(8,128)}, f32[1,1280]{1,0:T(1,128)}, f32[8,1024]{1,0:T(8,128)}, f32[8,1024]{1,0:T(8,128)}, /*index=5*/f32[1,8]{1,0:T(1,128)}) custom-call(bf16[1,257,1280]{2,1,0:T(8,128)(2,1)} %q_ref.1, bf16[1,257,1280]{2,1,0:T(8,128)(2,1)} %k_ref.1, bf16[1,257,1280]{2,1,0:T(8,128)(2,1)} %v_ref.1, ...), custom_call_target="tpu_custom_call" | custom-call | tf_op jit(solution)/shard_map/forward_pairs/pallas_call | solution.py:441
  32.2 6.9 %attention_back.1 = (bf16[1,257,1280]{2,1,0:T(8,128)(2,1)}, bf16[1,257,1280]{2,1,0:T(8,128)(2,1)}, bf16[1,257,1280]{2,1,0:T(8,128)(2,1)}, f32[8,1024]{1,0:T(8,128)}, f32[8,1024]{1,0:T(8,128)}, /*index=5*/f32[1,8]{1,0:T(1,128)}) custom-call(bf16[1,257,1280]{2,1,0:T(8,128)(2,1)} %q_ref.1, bf16[1,257,1280]{2,1,0:T(8,128)(2,1)} %k_ref.1, ...), custom_call_target="tpu_custom_call" | custom-call | tf_op jit(solution)/shard_map/attention_back/pallas_call | solution.py:493
